TPU v7x, 32 devices: a whole 2x2x4 slice. The times are simulated.
32 devices in a mesh: img: 8 (over z, x), band: 4 (over y, core).
Axes of the slice: x: 2, y: 2, z: 4, core: 2. Of those that a mesh axis runs over, the one named last changes fastest.
Arguments:
- images: bfloat16 [32, 32, 32, 512], P('img', 'band'), may hold values from -18 to 18
- cotangent: bfloat16 [32, 32, 32, 512], P('img', 'band'), may hold values from -6 to 6
- sizes: int32 [32], P('img'), may hold values from 16 to 32, as said below
- matrix_weight: float32 [5767168], P(('img', 'band')), may hold values from -0.8838835 to 0.8838835
- matrix_momentum: float32 [5767168], P(('img', 'band')), may hold values from -512 to 512
- matrix_average: float32 [5767168], P(('img', 'band')), may hold values from -0.8838835 to 0.8838835
- vector_weight: float32 [11, 512], replicated, may hold values from -0.3 to 1.45
- vector_momentum: float32 [11, 512], replicated, may hold values from -512 to 512
- vector_average: float32 [11, 512], replicated, may hold values from -0.3 to 1.45
Outputs:
- block_out: bfloat16 [32, 32, 32, 512], P('img', 'band')
- input_grad: float32 [32, 32, 32, 512], P('img', 'band')
- matrix_grads: float32 [5767168], P(('img', 'band'))
- matrix_moments: float32 [5767168], P(('img', 'band'))
- matrix_means: float32 [5767168], P(('img', 'band'))
- matrix_masters: float32 [5767168], P(('img', 'band'))
- vector_grads: float32 [11, 512], replicated
- vector_moments: float32 [11, 512], replicated
- vector_means: float32 [11, 512], replicated
- vector_masters: float32 [11, 512], replicated
Inputs may be any that keep to these rules, and one draw needn't show every extreme that they name: `sizes`: each value is 16, 24 or 32; among images 4 k to 4 k + 3 at least one has size 32.
All inputs are finite; a program needn't handle non-finite values.
Results may differ from a plain program's by a relative error of at most 0.013.
The roundings to bfloat16 on the way count: a program that leaves them out, or rounds other values in their place, can miss the bound.
Values may be sent and summed in bfloat16 or wider, within the bound.
No kernel may reach another device: no remote copies, remote signals or barrier semaphores. Data moves between devices by JAX's collectives and lax.ppermute only.
A program may use at most 192 MiB of HBM per device.

v0:
```python
import functools

import jax
import jax.numpy as jnp
from jax import lax
from jax.experimental import pallas as pl
from jax.experimental.pallas import tpu as pltpu
from jax.sharding import PartitionSpec as P

GROUPS = 32


EPS = 1e-06
MOMENTUM = 0.9
LR_MATRIX = 4e-05
LR_VECTOR = 0.0001
AVERAGE = 0.75


def extended(array, sides, width):
    for axis, dim in sides:
        count, length = (lax.axis_size(axis), array.shape[dim])
        up = [(i, (i + 1) % count) for i in range(count - 1)]
        down = [(j, i) for i, j in up]
        last = lax.slice_in_dim(array, length - width, length, axis=dim)
        initial = lax.slice_in_dim(array, 0, width, axis=dim)
        before = lax.ppermute(last, axis, up)
        after = lax.ppermute(initial, axis, down)
        array = jnp.concatenate([before, array, after], axis=dim)
    return array


def split_groups(field):
    return field.reshape(field.shape[:3] + (GROUPS, field.shape[3] // GROUPS))


def group_sums(field, mask):
    shaped = split_groups(field)
    weighted = shaped * mask[..., None]
    return (jnp.sum(weighted, axis=(1, 2, 4)), jnp.sum(weighted * shaped, axis=(1, 2, 4)))


def group_apply(field, sums, count, gain, shift):
    center = sums[0] / count[:, None]
    spread = sums[1] / count[:, None] - center * center
    scale = lax.rsqrt(spread + EPS)
    shaped = split_groups(field)
    normed = (shaped - center[:, None, None, :, None]) * scale[:, None, None, :, None]
    return normed.reshape(field.shape) * gain + shift


def normalize(field, mask, count, gain, shift):
    sums = lax.psum(group_sums(field, mask), "band")
    return (group_apply(field, sums, count, gain, shift), sums)


def normalize_back(field, sums, mask, count, gain, shift, upstream):
    _, pull = jax.vjp(
        lambda field_in, sums_in, gain_in, shift_in: group_apply(
            field_in, sums_in, count, gain_in, shift_in
        ),
        field,
        sums,
        gain,
        shift,
    )
    direct, grad_sums, grad_gain, grad_shift = pull(upstream)
    grad_sums = lax.psum(grad_sums, "band")
    _, pull_sums = jax.vjp(lambda field_in: group_sums(field_in, mask), field)
    return (direct + pull_sums(grad_sums)[0], grad_gain, grad_shift)


def activate(field, mask):
    return jax.nn.silu(field) * mask


def activate_back(field, mask, upstream):
    _, pull = jax.vjp(lambda inner: activate(inner, mask), field)
    return pull(upstream)[0]


def widen(field):
    return jnp.pad(field, ((0, 0), (0, 0), (1, 1), (0, 0)))


def taps(padded, kernel, height, width):
    total = jnp.zeros(padded.shape[:1] + (height, width, kernel.shape[2]), jnp.float32)
    for tap in range(9):
        row, column = (tap // 3, tap % 3)
        total = total + jnp.einsum(
            "ghwc,cd->ghwd",
            padded[:, row : row + height, column : column + width],
            kernel[tap],
            preferred_element_type=jnp.float32,
        )
    return total


def conv_forward(low_field, kernel):
    padded = widen(extended(low_field, (("band", 1),), 1))
    return (taps(padded, kernel, low_field.shape[1], low_field.shape[2]), padded)


def conv_backward(low_grad, kernel, padded):
    height, width = (low_grad.shape[1], low_grad.shape[2])
    grad_pad = widen(extended(low_grad, (("band", 1),), 1))
    flipped = jnp.swapaxes(kernel[::-1], 1, 2)
    grad_in = taps(grad_pad, flipped, height, width)
    pieces = []
    for tap in range(9):
        row, column = (tap // 3, tap % 3)
        pieces.append(
            jnp.einsum(
                "ghwc,ghwd->cd",
                padded[:, row : row + height, column : column + width],
                low_grad,
                preferred_element_type=jnp.float32,
            )
        )
    return (grad_in, jnp.stack(pieces))


def attend(query_low, key_full, key_valid, factor):
    score_matrix = (
        jnp.einsum("gqc,gkc->gqk", query_low, key_full, preferred_element_type=jnp.float32) * factor
    )
    score_matrix = jnp.where(key_valid[:, None, :], score_matrix, -1e30)
    top = jnp.max(score_matrix, axis=2, keepdims=True)
    raised = jnp.exp(score_matrix - top)
    total = jnp.sum(raised, axis=2, keepdims=True)
    return (raised / total, top, total)


def banded(
    images,
    cotangent,
    sizes,
    matrix_weight,
    matrix_momentum,
    matrix_average,
    vector_weight,
    vector_momentum,
    vector_average,
):
    batch, height, width, channels = images.shape
    square = channels * channels
    queries = height * width
    positions = width * width
    factor = channels ** (-0.5)
    weights = lax.all_gather(
        matrix_weight.astype(jnp.bfloat16), ("img", "band"), axis=0, tiled=True
    )
    kernel_one = weights[: 9 * square].reshape(9, channels, channels)
    kernel_two = weights[9 * square : 18 * square].reshape(9, channels, channels)
    attn_in = weights[18 * square : 21 * square].reshape(3, channels, channels)
    attention_output = weights[21 * square :].reshape(channels, channels)
    lines = lax.axis_index("band") * height + jnp.arange(height)
    across = jnp.arange(width)
    limit = sizes[:, None, None]
    inside = (lines[None, :, None] < limit) & (across[None, None, :] < limit)
    mask = jnp.where(inside, 1.0, 0.0).astype(jnp.float32)[..., None]
    count = (sizes * sizes * (channels // GROUPS)).astype(jnp.float32)
    spots = jnp.arange(positions)
    key_valid = ((spots // width)[None, :] < sizes[:, None]) & (
        (spots % width)[None, :] < sizes[:, None]
    )
    start = images.astype(jnp.float32) * mask
    norm_one, sums_one = normalize(start, mask, count, vector_weight[0], vector_weight[1])
    act_one = activate(norm_one, mask).astype(jnp.bfloat16)
    conv_raw, padded_one = conv_forward(act_one, kernel_one)
    conv_out = conv_raw + vector_weight[2]
    norm_two, sums_two = normalize(conv_out, mask, count, vector_weight[3], vector_weight[4])
    act_two = activate(norm_two, mask).astype(jnp.bfloat16)
    conv_raw, padded_two = conv_forward(act_two, kernel_two)
    resid = (start + conv_raw + vector_weight[5]) * mask
    norm_three, sums_three = normalize(resid, mask, count, vector_weight[6], vector_weight[7])
    normed = (norm_three * mask).astype(jnp.bfloat16).reshape(batch, queries, channels)
    projected = jnp.einsum("gqc,jcd->jgqd", normed, attn_in, preferred_element_type=jnp.float32)
    query_low = (projected[0] + vector_weight[8]).astype(jnp.bfloat16)
    key_low = projected[1].astype(jnp.bfloat16)
    value_low = (projected[2] + vector_weight[9]).astype(jnp.bfloat16)
    key_full, value_full = (
        lax.all_gather(key_low, "band", axis=1, tiled=True),
        lax.all_gather(value_low, "band", axis=1, tiled=True),
    )
    probability_rows, row_top, row_total = attend(query_low, key_full, key_valid, factor)
    mixed_values = jnp.einsum(
        "gqk,gkc->gqc",
        probability_rows.astype(jnp.bfloat16),
        value_full,
        preferred_element_type=jnp.float32,
    ).astype(jnp.bfloat16)
    output_rows = (
        jnp.einsum(
            "gqc,cd->gqd", mixed_values, attention_output, preferred_element_type=jnp.float32
        )
        + vector_weight[10]
    )
    block_out = ((resid + output_rows.reshape(images.shape)) * mask).astype(jnp.bfloat16)
    grad_top = cotangent.astype(jnp.float32) * mask
    grad_proj = grad_top.reshape(batch, queries, channels)
    grad_proj_low = grad_proj.astype(jnp.bfloat16)
    grad_out_weight = jnp.einsum(
        "gqc,gqd->cd", mixed_values, grad_proj_low, preferred_element_type=jnp.float32
    )
    grad_mixed = jnp.einsum(
        "gqd,cd->gqc", grad_proj_low, attention_output, preferred_element_type=jnp.float32
    ).astype(jnp.bfloat16)
    back_keys, back_values = (
        lax.all_gather(key_low, "band", axis=1, tiled=True),
        lax.all_gather(value_low, "band", axis=1, tiled=True),
    )
    back_probs = attend(query_low, back_keys, key_valid, factor)[0]
    grad_probs = jnp.einsum(
        "gqc,gkc->gqk", grad_mixed, back_values, preferred_element_type=jnp.float32
    )
    weighted_sum = jnp.sum(back_probs * grad_probs, axis=2, keepdims=True)
    grad_scores = back_probs * (grad_probs - weighted_sum)
    grad_scores_low = (grad_scores * factor).astype(jnp.bfloat16)
    grad_query = jnp.einsum(
        "gqk,gkc->gqc", grad_scores_low, back_keys, preferred_element_type=jnp.float32
    ).astype(jnp.bfloat16)
    key_terms = jnp.einsum(
        "gqk,gqc->gkc", grad_scores_low, query_low, preferred_element_type=jnp.float32
    )
    value_terms = jnp.einsum(
        "gqk,gqc->gkc",
        back_probs.astype(jnp.bfloat16),
        grad_mixed,
        preferred_element_type=jnp.float32,
    )
    grad_key, grad_value = (
        lax.psum_scatter(
            key_terms.astype(jnp.bfloat16), "band", scatter_dimension=1, tiled=True
        ).astype(jnp.float32),
        lax.psum_scatter(
            value_terms.astype(jnp.bfloat16), "band", scatter_dimension=1, tiled=True
        ).astype(jnp.float32),
    )
    grad_value_low = grad_value.astype(jnp.bfloat16)
    grads_low = jnp.stack([grad_query, grad_key.astype(jnp.bfloat16), grad_value_low])
    grad_in_weights = jnp.einsum(
        "gqc,jgqd->jcd", normed, grads_low, preferred_element_type=jnp.float32
    )
    grad_normed = (
        jnp.einsum("jgqd,jcd->gqc", grads_low, attn_in, preferred_element_type=jnp.float32).reshape(
            images.shape
        )
        * mask
    )
    grad_resid_norm, grad_gain_three, grad_shift_three = normalize_back(
        resid, sums_three, mask, count, vector_weight[6], vector_weight[7], grad_normed
    )
    grad_resid = (grad_top + grad_resid_norm) * mask
    grad_act_two, grad_kernel_two = conv_backward(
        grad_resid.astype(jnp.bfloat16), kernel_two, padded_two
    )
    grad_norm_two = activate_back(norm_two, mask, grad_act_two)
    grad_conv_out, grad_gain_two, grad_shift_two = normalize_back(
        conv_out, sums_two, mask, count, vector_weight[3], vector_weight[4], grad_norm_two
    )
    grad_act_one, grad_kernel_one = conv_backward(
        grad_conv_out.astype(jnp.bfloat16), kernel_one, padded_one
    )
    grad_norm_one = activate_back(norm_one, mask, grad_act_one)
    grad_start, grad_gain_one, grad_shift_one = normalize_back(
        start, sums_one, mask, count, vector_weight[0], vector_weight[1], grad_norm_one
    )
    input_grad = (grad_resid + grad_start) * mask
    vector_terms = jnp.stack(
        [
            grad_gain_one,
            grad_shift_one,
            jnp.sum(grad_conv_out, axis=(0, 1, 2)),
            grad_gain_two,
            grad_shift_two,
            jnp.sum(grad_resid, axis=(0, 1, 2)),
            grad_gain_three,
            grad_shift_three,
            jnp.sum(grad_query, axis=(0, 1), dtype=jnp.float32),
            jnp.sum(grad_value_low, axis=(0, 1), dtype=jnp.float32),
            jnp.sum(grad_proj, axis=(0, 1)),
        ]
    )
    vector_grads = lax.psum(vector_terms, ("img", "band"))
    grad_flat = jnp.concatenate(
        [
            grad_kernel_one.reshape(-1),
            grad_kernel_two.reshape(-1),
            grad_in_weights.reshape(-1),
            grad_out_weight.reshape(-1),
        ]
    )
    matrix_grads = lax.psum_scatter(grad_flat, ("img", "band"), scatter_dimension=0, tiled=True)
    matrix_moments = MOMENTUM * matrix_momentum + matrix_grads
    matrix_masters = matrix_weight - LR_MATRIX * (matrix_grads + MOMENTUM * matrix_moments)
    matrix_means = AVERAGE * matrix_average + (1.0 - AVERAGE) * matrix_masters
    vector_moments = MOMENTUM * vector_momentum + vector_grads
    vector_masters = vector_weight - LR_VECTOR * (vector_grads + MOMENTUM * vector_moments)
    vector_means = AVERAGE * vector_average + (1.0 - AVERAGE) * vector_masters
    return (
        block_out,
        input_grad,
        matrix_grads,
        matrix_moments,
        matrix_means,
        matrix_masters,
        vector_grads,
        vector_moments,
        vector_means,
        vector_masters,
    )


F32 = jnp.float32
BF16 = jnp.bfloat16
SIDE = 32
VMEM_LIMIT = 58 * 1024 * 1024


def dot(a, b):
    return lax.dot_general(a, b, (((1,), (0,)), ((), ())), preferred_element_type=F32)


def dot_nt(a, b):
    return lax.dot_general(a, b, (((1,), (1,)), ((), ())), preferred_element_type=F32)


def dot_tn(a, b):
    return lax.dot_general(a, b, (((0,), (0,)), ((), ())), preferred_element_type=F32)


def call(body, outs, ins, scratch=(), flops=0, name=None, aliases=None):
    spaces = {"v": pl.BlockSpec(memory_space=pltpu.VMEM), "s": pl.BlockSpec(memory_space=pltpu.SMEM),
              "a": pl.BlockSpec(memory_space=pl.ANY)}
    return pl.pallas_call(
        body,
        out_shape=[o for o, _ in outs],
        in_specs=[spaces[s] for _, s in ins],
        out_specs=[spaces[s] for _, s in outs],
        scratch_shapes=list(scratch),
        input_output_aliases=aliases or {},
        compiler_params=pltpu.CompilerParams(vmem_limit_bytes=VMEM_LIMIT),
        cost_estimate=pl.CostEstimate(flops=flops, bytes_accessed=0, transcendentals=0),
        name=name,
    )(*[a for a, _ in ins])


def shape(dims, dtype):
    return jax.ShapeDtypeStruct(dims, dtype)


def fold(x):
    return jnp.sum(x.reshape(x.shape[0] // 8, 8, x.shape[1]), axis=0)


def group_total(x):
    lane = lax.broadcasted_iota(jnp.int32, x.shape, 1)
    width = x.shape[1]
    for s in (1, 2, 4, 8):
        up = pltpu.roll(x, width - s, 1)
        down = pltpu.roll(x, s, 1)
        x = x + jnp.where((lane & s) == 0, up, down)
    return x


def total_of(*parts):
    rows = [jnp.sum(p, axis=0, keepdims=True) for p in parts]
    pad = jnp.zeros((8 - len(rows), rows[0].shape[1]), F32)
    return jnp.concatenate(rows + [pad], axis=0)


def moments(s1, s2, size):
    count = (size * size * 16).astype(F32)
    both = group_total(total_of(s1, s2)) / count
    mean = both[0:1]
    spread = both[1:2] - mean * mean
    return mean, lax.rsqrt(spread + EPS)


def row_mask(size, channels):
    across = lax.broadcasted_iota(jnp.int32, (SIDE, channels), 0)
    inside = across < size
    return lambda h: inside & (h < size)


def sigmoid(y):
    return 0.5 * jnp.tanh(0.5 * y) + 0.5


def rows(h):
    return pl.ds(pl.multiple_of(h * SIDE, SIDE), SIDE)


def put_shifted(ref, h, r, forward):
    channels = r.shape[1]
    w = lax.broadcasted_iota(jnp.int32, r.shape, 0)
    before = jnp.where(w == 0, 0.0, pltpu.roll(r, 1, 0)).astype(BF16)
    after = jnp.where(w == SIDE - 1, 0.0, pltpu.roll(r, SIDE - 1, 0)).astype(BF16)
    first, last = (before, after) if forward else (after, before)
    at = pl.ds(pl.multiple_of((h + 1) * SIDE, SIDE), SIDE)
    ref[at, 0:channels] = first
    ref[at, channels : 2 * channels] = r.astype(BF16)
    ref[at, 2 * channels :] = last


def clear_border(ref):
    zero = jnp.zeros((SIDE, ref.shape[1]), BF16)
    ref[0:SIDE, :] = zero
    ref[(SIDE + 1) * SIDE :, :] = zero


def put_transposed(ref, src_ref, row0, lane0):
    channels, count = ref.shape
    for j in range(count // 256):
        block = src_ref[row0 + j * 256 : row0 + (j + 1) * 256, lane0 : lane0 + channels]
        ref[:, j * 256 : (j + 1) * 256] = block.T


def act_one_body(size_ref, img_ref, vec_ref, pad_ref, at_ref, stat_ref):
    size = size_ref[0]
    channels = img_ref.shape[1]
    mask = row_mask(size, channels)

    def sums(h, carry):
        x = jnp.where(mask(h), img_ref[rows(h), :].astype(F32), 0.0)
        return carry[0] + fold(x), carry[1] + fold(x * x)

    zero = jnp.zeros((8, channels), F32)
    s1, s2 = lax.fori_loop(0, SIDE, sums, (zero, zero), unroll=2)
    mean, scale = moments(s1, s2, size)
    stat_ref[0:1, :] = mean
    stat_ref[1:2, :] = scale
    stat_ref[2:8, :] = jnp.zeros((6, channels), F32)
    apply_norm(img_ref, mean, scale * vec_ref[0:1, :], vec_ref[1:2, :], mask, pad_ref)
    put_transposed(at_ref, pad_ref, SIDE, 0)


def apply_norm(src_ref, mean, scale, shift, mask, pad_ref):
    clear_border(pad_ref)

    def apply(h, carry):
        y = (src_ref[rows(h), :].astype(F32) - mean) * scale + shift
        at = pl.ds(pl.multiple_of((h + 1) * SIDE, SIDE), SIDE)
        pad_ref[at, :] = jnp.where(mask(h), y * sigmoid(y), 0.0).astype(BF16)
        return carry

    lax.fori_loop(0, SIDE, apply, 0, unroll=4)


def act_one(size, img, vec):
    n, c = img.shape
    return call(act_one_body,
        [(shape((n + 64, c), BF16), "v"), (shape((c, n), BF16), "v"), (shape((8, c), F32), "v")],
        [(size, "s"), (img, "v"), (vec, "v")], name="act_one")


MB = 256


def start_copies(src_ref, dst_ref, sems, parts, offset=0):
    length = dst_ref.shape[0] // parts
    copies = [
        pltpu.make_async_copy(src_ref.at[pl.ds(offset + p * length, length)], dst_ref.at[pl.ds(p * length, length)], sems.at[p])
        for p in range(parts)
    ]
    for copy in copies:
        copy.start()
    return copies


COLUMNS = (1, 0, 2)


def start_kernel(src_ref, dst_ref, sems, offset):
    c = dst_ref.shape[1]
    copies = {}
    for dx in COLUMNS:
        for dy in range(3):
            tap = 3 * dy + dx
            copies[tap] = pltpu.make_async_copy(
                src_ref.at[pl.ds(offset + tap * c, c)], dst_ref.at[pl.ds(tap * c, c)], sems.at[tap]
            )
            copies[tap].start()
    return copies


def conv(pad_ref, k_ref, copies, out_ref, mb, finish):
    n, c = out_ref.shape
    zero = jnp.zeros((8, c), F32)
    carry = (zero, zero)
    across = lax.broadcasted_iota(jnp.int32, (mb, c), 0) & (SIDE - 1)
    for dx in COLUMNS:
        for dy in range(3):
            copies[3 * dy + dx].wait()

        def block(m, carry, dx=dx):
            first = pl.multiple_of(m * mb, mb)
            at = pl.ds(first, mb)
            value = None
            for dy in range(3):
                tap = 3 * dy + dx
                term = dot(pad_ref[pl.ds(first + dy * SIDE, mb), :], k_ref[tap * c : (tap + 1) * c, :])
                value = term if value is None else value + term
            if dx == 0:
                value = jnp.where(across == 0, 0.0, pltpu.roll(value, 1, 0))
            if dx == 2:
                value = jnp.where(across == SIDE - 1, 0.0, pltpu.roll(value, mb - 1, 0))
            if dx != COLUMNS[0]:
                value = value + out_ref[at, :]
            if dx == COLUMNS[-1]:
                value, carry = finish(first, value, carry)
            out_ref[at, :] = value
            return carry

        carry = lax.fori_loop(0, n // mb, block, carry, unroll=4)
    return carry


def pixel_mask(size, first, count, c):
    place = lax.broadcasted_iota(jnp.int32, (count, c), 0) + first
    return ((place >> 5) < size) & ((place & (SIDE - 1)) < size)


def put_stats(stat_ref, mean, scale):
    stat_ref[...] = jnp.concatenate([mean, scale, jnp.zeros((6, mean.shape[1]), F32)], axis=0)


def pieces_of(row, count, half):
    found = []
    for spot in range(row // half, (row + count - 1) // half + 1):
        found.append((spot, max(row, spot * half), min(row + count, (spot + 1) * half)))
    return found


def send_rows(stage, base, row, count, at_ref, rounds, sem):
    half = rounds[-1][0].shape[1]
    for spot, lo, hi in pieces_of(row, count, half):
        owner, tail = spot // 2, spot % 2
        refs, inner = rounds[owner // 16], owner % 16
        z, x, y, c = inner // 8, (inner >> 2) & 1, (inner >> 1) & 1, inner & 1
        index = ((at_ref[1] ^ x) * 2 + (at_ref[2] ^ y)) * 2 + z
        source = stage.at[pl.ds(base + lo - row, hi - lo)]
        place = pl.ds(lo - spot * half, hi - lo)
        for other in range(2):

            @pl.when((at_ref[3] ^ c) == other)
            def _(ref=refs[2 * other + tail], source=source, place=place):
                pltpu.make_async_copy(source, ref.at[index, place], sem).start()

    return pltpu.make_async_copy(stage.at[pl.ds(base, count)], stage.at[pl.ds(base, count)], sem)


QB = 256
PB = 256


def forward_body(
    at_ref, pad_one_ref, vec_ref, w_any, img_any, cot_any,
    conv_any, stat_two_ref, mixed_any, resid_any, grad_any, e3_any, vout_ref, *refs,
):
    high, low = refs[0:4], refs[4:8]
    (k_one, k_two, w_ref, img_ref, cot_ref, conv_ref, pad_ref, act_t, resid_ref, normed_ref, normed_t,
     q_ref, k_ref, v_ref, p_ref, ds_ref, mixed_ref, top_ref, gm_ref, gq_ref, gk_ref, gv_ref, grad_ref, e3_ref, gw_ref,
     one_sems, two_sems, w_sems, in_sems, out_sems, gw_sem, gk_sems) = refs[8:]
    n, c = normed_ref.shape
    size = at_ref[0]
    one_copies = start_kernel(w_any, k_one, one_sems, 0)
    two_copies = start_kernel(w_any, k_two, two_sems, 9 * c)
    img_copy = pltpu.make_async_copy(img_any, img_ref, in_sems.at[0])
    cot_copy = pltpu.make_async_copy(cot_any, cot_ref, in_sems.at[1])
    img_copy.start()
    w_copies = start_copies(w_any, w_ref, w_sems, 4, 18 * c)
    cot_copy.start()
    leaving = []

    def leave(src, dst):
        copy = pltpu.make_async_copy(src, dst, out_sems.at[len(leaving)])
        copy.start()
        leaving.append(copy)

    mask = row_mask(size, c)
    zero = jnp.zeros((8, c), F32)

    bias_one = vec_ref[2:3, :]

    def finish_one(first, v, carry):
        v = v + bias_one
        x = jnp.where(pixel_mask(size, first, MB, c), v, 0.0)
        return v, (carry[0] + fold(x), carry[1] + fold(x * x))

    s1, s2 = conv(pad_one_ref, k_one, one_copies, conv_ref, MB, finish_one)
    leave(conv_ref, conv_any)
    mean, scale = moments(s1, s2, size)
    put_stats(stat_two_ref, mean, scale)
    apply_norm(conv_ref, mean, scale * vec_ref[3:4, :], vec_ref[4:5, :], mask, pad_ref)
    put_transposed(act_t, pad_ref, SIDE, 0)

    bias_two = vec_ref[5:6, :]
    img_copy.wait()

    def finish_two(first, v, carry):
        v = v + bias_two + img_ref[pl.ds(first, MB), :].astype(F32)
        x = jnp.where(pixel_mask(size, first, MB, c), v, 0.0)
        return x, (carry[0] + fold(x), carry[1] + fold(x * x))

    s1, s2 = conv(pad_ref, k_two, two_copies, resid_ref, MB, finish_two)
    leave(resid_ref, resid_any)
    mean, scale = moments(s1, s2, size)
    gain = vec_ref[6:7, :]
    full_gain, shift = scale * gain, vec_ref[7:8, :]
    cot_copy.wait()

    def apply(h, carry):
        y = (resid_ref[rows(h), :] - mean) * full_gain + shift
        normed_ref[rows(h), :] = jnp.where(mask(h), y, 0.0).astype(BF16)
        t = jnp.where(mask(h), cot_ref[rows(h), :].astype(F32), 0.0)
        top_ref[rows(h), :] = t.astype(BF16)
        return carry + fold(t)

    top_sum = lax.fori_loop(0, SIDE, apply, zero, unroll=4)
    put_transposed(normed_t, normed_ref, 0, 0)

    for copy in w_copies:
        copy.wait()
    factor = c ** (-0.5)
    wq, wk, wv, wo = (functools.partial(lambda j: w_ref[j * c : (j + 1) * c, :], j) for j in range(4))
    qb, vb = vec_ref[8:9, :], vec_ref[9:10, :]
    def project(m, carry):
        at = pl.ds(pl.multiple_of(m * PB, PB), PB)
        x = normed_ref[at, :]
        q_ref[at, :] = (dot(x, wq()) + qb).astype(BF16)
        k_ref[at, :] = dot(x, wk()).astype(BF16)
        v_ref[at, :] = (dot(x, wv()) + vb).astype(BF16)
        gm_ref[at, :] = dot_nt(top_ref[at, :], wo()).astype(BF16)
        return carry

    lax.fori_loop(0, n // PB, project, 0, unroll=2)

    spot = lax.broadcasted_iota(jnp.int32, (1, n), 1)
    key_bias = jnp.where(((spot >> 5) < size) & ((spot & (SIDE - 1)) < size), 0.0, -1e30)

    def queries(m, carry):
        at = pl.ds(pl.multiple_of(m * QB, QB), QB)
        s = dot_nt(q_ref[at, :], k_ref[...]) * factor + key_bias
        raised = jnp.exp(s - jnp.max(s, axis=1, keepdims=True))
        p = raised * (1.0 / jnp.sum(raised, axis=1, keepdims=True))
        low_p = p.astype(BF16)
        p_ref[at, :] = low_p
        mixed_ref[at, :] = dot(low_p, v_ref[...]).astype(BF16)
        gp = dot_nt(gm_ref[at, :], v_ref[...])
        weighted = jnp.sum(p * gp, axis=1, keepdims=True)
        ds = (p * ((gp - weighted) * factor)).astype(BF16)
        ds_ref[at, :] = ds
        gq_ref[at, :] = dot(ds, k_ref[...]).astype(BF16)
        return carry

    lax.fori_loop(0, n // QB, queries, 0)
    leave(mixed_ref, mixed_any)

    def keys(m, carry):
        at = pl.ds(pl.multiple_of(m * QB, QB), QB)
        gk_ref[at, :] = dot_tn(ds_ref[:, at], q_ref[...]).astype(BF16)
        gv_ref[at, :] = dot_tn(p_ref[:, at], gm_ref[...]).astype(BF16)
        return carry

    lax.fori_loop(0, n // QB, keys, 0)
    gw_ref[0:c, :] = dot(normed_t[...], gq_ref[...]).astype(BF16)
    gw_ref[c : 2 * c, :] = dot(normed_t[...], gk_ref[...]).astype(BF16)
    gw_ref[2 * c : 3 * c, :] = dot(normed_t[...], gv_ref[...]).astype(BF16)
    gw_ref[3 * c : 4 * c, :] = dot_tn(mixed_ref[...], top_ref[...]).astype(BF16)
    waits = [send_rows(gw_ref, 0, 18 * c, 4 * c, at_ref, (None, high), gw_sem)]

    def normed_grad(m, carry):
        su, sux, sq, sv = carry
        first = pl.multiple_of(m * PB, PB)
        at = pl.ds(first, PB)
        gq, gk, gv = gq_ref[at, :], gk_ref[at, :], gv_ref[at, :]
        u = dot_nt(gq, wq()) + dot_nt(gk, wk()) + dot_nt(gv, wv())
        u = jnp.where(pixel_mask(size, first, PB, c), u, 0.0)
        grad_ref[at, :] = u
        xhat = (resid_ref[at, :] - mean) * scale
        return su + fold(u), sux + fold(u * xhat), sq + fold(gq.astype(F32)), sv + fold(gv.astype(F32))

    su, sux, sq, sv = lax.fori_loop(0, n // PB, normed_grad, (zero, zero, zero, zero), unroll=2)
    count = (size * size * 16).astype(F32)
    both = group_total(total_of(su, sux) * gain) / count
    m1, m2 = both[0:1], both[1:2]
    clear_border(e3_ref)

    def back(h, carry):
        xhat = (resid_ref[rows(h), :] - mean) * scale
        g = (grad_ref[rows(h), :] * gain - m1 - xhat * m2) * scale + top_ref[rows(h), :].astype(F32)
        g = jnp.where(mask(h), g, 0.0)
        grad_ref[rows(h), :] = g
        put_shifted(e3_ref, h, g.astype(BF16).astype(F32), False)
        return carry + fold(g)

    sg = lax.fori_loop(0, SIDE, back, zero, unroll=2)
    leave(e3_ref, e3_any)
    leave(grad_ref, grad_any)
    vout_ref[...] = total_of(sg, sux, su, sq, sv, top_sum)
    waits += kernel_gradient(act_t, e3_ref, k_one, 9 * c, at_ref, (low, high), gk_sems)
    for wait in waits + leaving:
        wait.wait()


def forward(at, pad_one, vec, weights, img, cot):
    n, c = img.shape
    half = (shape((8, weights.shape[0] // 64, c), BF16), "a")

    def low(*dims):
        return pltpu.VMEM(dims, BF16)

    full = low(n, c)
    found = call(forward_body,
        [(shape((n, c), F32), "a"), (shape((8, c), F32), "v"), (shape((n, c), BF16), "a"), (shape((n, c), F32), "a"),
         (shape((n, c), F32), "a"), (shape((n + 2 * SIDE, 3 * c), BF16), "a"), (shape((8, c), F32), "v")] + [half] * 8,
        [(at, "s"), (pad_one, "v"), (vec, "v"), (weights, "a"), (img, "a"), (cot, "a")],
        [low(9 * c, c), low(9 * c, c), low(4 * c, c), full, full, pltpu.VMEM((n, c), F32), low(n + 2 * SIDE, c), low(c, n),
         pltpu.VMEM((n, c), F32), full, low(c, n), full, full, full, low(n, n), low(n, n), full, full, full, full, full, full,
         pltpu.VMEM((n, c), F32), low(n + 2 * SIDE, 3 * c), low(4 * c, c),
         pltpu.SemaphoreType.DMA((9,)), pltpu.SemaphoreType.DMA((9,)), pltpu.SemaphoreType.DMA((4,)),
         pltpu.SemaphoreType.DMA((2,)), pltpu.SemaphoreType.DMA((5,)), pltpu.SemaphoreType.DMA, pltpu.SemaphoreType.DMA((9,))],
        name="forward")
    return found[:7], found[7:11], found[11:15]


def out_body(at_ref, mixed_ref, resid_ref, vec_ref, w_any, out_ref, wo_ref, sem):
    n, c = mixed_ref.shape
    copy = pltpu.make_async_copy(w_any.at[pl.ds(21 * c, c)], wo_ref, sem)
    copy.start()
    copy.wait()
    for m in range(n // MB):
        at = slice(m * MB, (m + 1) * MB)
        value = dot(mixed_ref[at, :], wo_ref[...]) + vec_ref[10:11, :] + resid_ref[at, :]
        out_ref[at, :] = jnp.where(pixel_mask(at_ref[0], m * MB, MB, c), value, 0.0).astype(BF16)


def block_rows(at, mixed, resid, vec, weights):
    n, c = mixed.shape
    return call(out_body, [(shape((n, c), BF16), "v")],
        [(at, "s"), (mixed, "v"), (resid, "v"), (vec, "v"), (weights, "a")],
        [pltpu.VMEM((c, c), BF16), pltpu.SemaphoreType.DMA], name="block_rows")[0]


def kernel_gradient(act_t, e3_ref, stage, row, at_ref, rounds, sems):
    c, n = act_t.shape

    def one_row(dy, carry):
        lo = pl.multiple_of((2 - dy) * SIDE, SIDE)
        for dx in range(3):
            value = dot(act_t[...], e3_ref[pl.ds(lo, n), dx * c : (dx + 1) * c])
            stage[pl.ds(pl.multiple_of((3 * dy + dx) * c, c), c), :] = value.astype(BF16)
        for now in range(3):

            @pl.when(dy == now)
            def _(now=now):
                send_rows(stage, 3 * now * c, row + 3 * now * c, 3 * c, at_ref, rounds, sems.at[now])

        return carry

    lax.fori_loop(0, 3, one_row, 0, unroll=1)
    places = [stage.at[pl.ds(3 * dy * c, 3 * c)] for dy in range(3)]
    return [pltpu.make_async_copy(place, place, sems.at[dy]) for dy, place in enumerate(places)]


def conv_back(e3_ref, k_ref, copies, out_ref):
    n, c = out_ref.shape
    for dy in range(3):
        copies[dy].wait()
        lo = (2 - dy) * SIDE

        def block(m, carry, dy=dy, lo=lo):
            first = pl.multiple_of(m * MB, MB)
            value = None
            for dx in range(3):
                tap = 3 * dy + dx
                term = dot_nt(e3_ref[pl.ds(first + lo, MB), dx * c : (dx + 1) * c], k_ref[tap * c : (tap + 1) * c, :])
                value = term if value is None else value + term
            if dy > 0:
                value = value + out_ref[pl.ds(first, MB), :]
            out_ref[pl.ds(first, MB), :] = value
            return carry

        lax.fori_loop(0, n // MB, block, 0, unroll=4)


def norm_back_sums(src_ref, g_ref, mean, scale, gain, shift, mask, size):
    c = g_ref.shape[1]

    def sums(h, carry):
        xhat = (src_ref[rows(h), :].astype(F32) - mean) * scale
        y = xhat * gain + shift
        s = sigmoid(y)
        u = jnp.where(mask(h), g_ref[rows(h), :] * (s * (1.0 + y * (1.0 - s))), 0.0)
        g_ref[rows(h), :] = u
        return carry[0] + fold(u), carry[1] + fold(u * xhat)

    zero = jnp.zeros((8, c), F32)
    su, sux = lax.fori_loop(0, SIDE, sums, (zero, zero), unroll=2)
    count = (size * size * 16).astype(F32)
    both = group_total(total_of(su, sux) * gain) / count
    return su, sux, both[0:1], both[1:2]


def back_two_body(
    at_ref, e3_ref, vec_ref, stat_ref, k_any, conv_any, act_any, i0, i1, i2, i3,
    e3_any, vout_ref, o0, o1, o2, o3, g_ref, conv_ref, act_t, e3_out, k_vmem, sems, in_sems, out_sem, gk_sems,
):
    n, c = conv_ref.shape
    copies = start_copies(k_any, k_vmem, sems, 3, 9 * c)
    conv_copy = pltpu.make_async_copy(conv_any, conv_ref, in_sems.at[0])
    act_copy = pltpu.make_async_copy(act_any, act_t, in_sems.at[1])
    conv_copy.start()
    act_copy.start()
    size = at_ref[0]
    mask = row_mask(size, c)
    conv_back(e3_ref, k_vmem, copies, g_ref)
    conv_copy.wait()
    mean, scale = stat_ref[0:1, :], stat_ref[1:2, :]
    gain, shift = vec_ref[3:4, :], vec_ref[4:5, :]
    su, sux, m1, m2 = norm_back_sums(conv_ref, g_ref, mean, scale, gain, shift, mask, size)
    clear_border(e3_out)

    def apply(h, carry):
        xhat = (conv_ref[rows(h), :] - mean) * scale
        g = jnp.where(mask(h), (g_ref[rows(h), :] * gain - m1 - xhat * m2) * scale, 0.0)
        put_shifted(e3_out, h, g.astype(BF16).astype(F32), False)
        return carry + fold(g)

    sg = lax.fori_loop(0, SIDE, apply, jnp.zeros((8, c), F32), unroll=2)
    leaving = pltpu.make_async_copy(e3_out, e3_any, out_sem)
    leaving.start()
    vout_ref[...] = total_of(sg, sux, su)
    act_copy.wait()
    for wait in kernel_gradient(act_t, e3_out, k_vmem, 0, at_ref, ((o0, o1, o2, o3),), gk_sems):
        wait.wait()
    leaving.wait()


def back_two(at, e3, weights, vec, conv_out, stat, act, low):
    n, c = conv_out.shape
    half = shape(low[0].shape, BF16)
    e3_out, vout, *low = call(back_two_body,
        [(shape((n + 64, 3 * c), BF16), "a"), (shape((8, c), F32), "v")] + [(half, "a")] * 4,
        [(at, "s"), (e3, "v"), (vec, "v"), (stat, "v"), (weights, "a"), (conv_out, "a"), (act, "a")] + [(v, "a") for v in low],
        [pltpu.VMEM((n, c), F32), pltpu.VMEM((n, c), F32), pltpu.VMEM((c, n), BF16), pltpu.VMEM((n + 64, 3 * c), BF16),
         pltpu.VMEM((9 * c, c), BF16), pltpu.SemaphoreType.DMA((3,)), pltpu.SemaphoreType.DMA((2,)), pltpu.SemaphoreType.DMA,
         pltpu.SemaphoreType.DMA((9,))],
        name="back_two", aliases={7 + i: 2 + i for i in range(4)})
    return e3_out, vout, low


def back_one_body(
    size_ref, e3_ref, k_ref, vec_ref, img_ref, stat_ref, resid_ref, rows_ref, both_any, vout_ref,
    g_ref, out_ref, k_vmem, sems, rows_sem, out_sem,
):
    n, c = img_ref.shape
    copies = start_copies(k_ref, k_vmem, sems, 3)
    bands, quarter = both_any.shape[0], both_any.shape[2]
    kept = [pltpu.make_async_copy(rows_ref.at[pl.ds(j * quarter, quarter)], both_any.at[j, 0], rows_sem.at[j]) for j in range(bands)]
    for copy in kept:
        copy.start()
    size = size_ref[0]
    mask = row_mask(size, c)
    conv_back(e3_ref, k_vmem, copies, g_ref)
    mean, scale = stat_ref[0:1, :], stat_ref[1:2, :]
    gain, shift = vec_ref[0:1, :], vec_ref[1:2, :]
    su, sux, m1, m2 = norm_back_sums(img_ref, g_ref, mean, scale, gain, shift, mask, size)

    def apply(h, carry):
        xhat = (img_ref[rows(h), :].astype(F32) - mean) * scale
        g = (g_ref[rows(h), :] * gain - m1 - xhat * m2) * scale + resid_ref[rows(h), :]
        out_ref[rows(h), :] = jnp.where(mask(h), g, 0.0).astype(out_ref.dtype)
        return carry

    lax.fori_loop(0, SIDE, apply, 0, unroll=2)
    for j in range(bands):
        copy = pltpu.make_async_copy(out_ref.at[pl.ds(j * quarter, quarter)], both_any.at[j, 1], out_sem.at[j])
        copy.start()
        kept.append(copy)
    vout_ref[...] = total_of(sux, su)
    for copy in kept:
        copy.wait()


def back_one(at, e3, weights, vec, img, stat, grad_resid, out, bands):
    n, c = img.shape
    return call(back_one_body, [(shape((bands, 2, n // bands, c), BF16), "a"), (shape((8, c), F32), "v")],
        [(at, "s"), (e3, "v"), (weights, "a"), (vec, "v"), (img, "v"), (stat, "v"), (grad_resid, "v"), (out, "v")],
        [pltpu.VMEM((n, c), F32), pltpu.VMEM((n, c), BF16), pltpu.VMEM((9 * c, c), BF16), pltpu.SemaphoreType.DMA((3,)),
         pltpu.SemaphoreType.DMA((bands,)), pltpu.SemaphoreType.DMA((bands,))],
        name="back_one")


ALL = ("img", "band")
CORE = [(b, b ^ 1) for b in range(4)]
ACROSS_Y = [(b, b ^ 2) for b in range(4)]
ACROSS_X = [(i, i ^ 1) for i in range(8)]

def after(value, *earlier, flops=0):
    def body(*refs):
        pass

    anywhere = pl.BlockSpec(memory_space=pl.ANY)
    return pl.pallas_call(
        body,
        out_shape=shape(value.shape, value.dtype),
        in_specs=[anywhere] * (1 + len(earlier)),
        out_specs=anywhere,
        input_output_aliases={0: 0},
        cost_estimate=pl.CostEstimate(flops=flops, bytes_accessed=0, transcendentals=0),
        name="after",
    )(value, *earlier)


def wide(*parts):
    total = parts[0].astype(F32)
    for part in parts[1:]:
        total = total + part.astype(F32)
    return total


def chip_sends(arrays, *earlier):
    mine_a, mine_b, theirs_a, theirs_b = arrays
    half, c = mine_a.shape[1:]
    dims = (2, 2, 2, half, c)
    if earlier:
        theirs_a, theirs_b = after(theirs_a, *earlier), after(theirs_b, *earlier)
    got = [lax.ppermute(v, "band", CORE) for v in (theirs_a, theirs_b)]
    pair_a = (mine_a.reshape(dims), got[0].reshape(dims))
    pair_b = (mine_b.reshape(dims), got[1].reshape(dims))
    send_a = wide(*(v[1] for v in pair_a)).astype(BF16)
    send_b = wide(*(v[:, 1] for v in pair_b)).astype(BF16)
    return pair_a, pair_b, send_a, send_b


def plane_swap(send_a, send_b):
    return lax.ppermute(send_a, "img", ACROSS_X), lax.ppermute(send_b, "band", ACROSS_Y)


def plane_sends(pair_a, pair_b, got_a, got_b):
    next_a = wide(*(v[0, 1] for v in pair_a), got_a[1]).astype(BF16)
    next_b = wide(*(v[1, 0] for v in pair_b), got_b[1]).astype(BF16)
    kept_a = (*(v[0, 0] for v in pair_a), got_a[0])
    kept_b = (*(v[0, 0] for v in pair_b), got_b[0])
    return kept_a, kept_b, next_a, next_b


def plane_sums(kept_a, kept_b, next_a, next_b, *earlier):
    last_a = lax.ppermute(next_a, "band", ACROSS_Y)
    last_b = lax.ppermute(next_b, "img", ACROSS_X)
    if earlier:
        last_a, last_b = after(last_a, *earlier), after(last_b, *earlier)
    return jnp.concatenate([wide(*kept_a, last_a), wide(*kept_b, last_b)], axis=1)


def owner_parts(low, high):
    z = lax.axis_index("img") // 2

    def block_of(plane):
        found = high[1]
        for at, block in ((2, high[0]), (1, low[1]), (0, low[0])):
            found = jnp.where(plane == at, block, found)
        return found

    sent = [block_of(z ^ step).astype(BF16) for step in (1, 2, 3)]
    got = [lax.ppermute(v, "img", [(i, i ^ (2 * step)) for i in range(8)]) for v, step in zip(sent, (1, 2, 3))]
    return [block_of(z)] + got, sent


def four_sum(v, axis, steps):
    a, b, c = (lax.ppermute(v, axis, [(i, i ^ step) for i in range(lax.axis_size(axis))]) for step in steps)
    return (v + a) + (b + c)


def whole_image(
    images,
    cotangent,
    sizes,
    matrix_weight,
    matrix_momentum,
    matrix_average,
    vector_weight,
    vector_momentum,
    vector_average,
):
    batch, height, width, c = images.shape
    n = width * width
    mine = lax.axis_index("band")
    place = lax.axis_index("img")
    at = jnp.stack([lax.dynamic_index_in_dim(sizes, mine, 0, False), place % 2, mine // 2, mine % 2])

    def to_image(field):
        parts = field.reshape(batch, height * width, c)
        return lax.all_to_all(parts, "band", 0, 0, tiled=True).reshape(n, c)

    weights = lax.all_gather(matrix_weight.astype(BF16).reshape(-1, c), ALL, axis=0, tiled=True)
    img = to_image(images)
    cot = to_image(cotangent)
    pad_one, act_t, stat_one = act_one(at, img, vector_weight)
    (conv_out, stat_two, mixed, resid, grad_resid, e3_two, v3), high, low = forward(
        at, pad_one, vector_weight, weights, img, cot
    )
    high = chip_sends(high)
    out = block_rows(at, mixed, resid, vector_weight, weights)
    e3_two = after(e3_two, high[2], high[3], out)
    swapped = plane_swap(high[2], high[3])
    e3_one, v2, low = back_two(at, e3_two, weights, vector_weight, conv_out, stat_two, act_t, low)
    low = chip_sends(low, *swapped)
    high = plane_sends(*high[:2], *swapped)
    low_sends = low[2:4]
    e3_one = after(e3_one, *low_sends)
    swapped = plane_swap(low[2], low[3])
    both, v1 = back_one(at, e3_one, weights, vector_weight, img, stat_one, grad_resid, out, batch)
    vecs = jnp.stack([v1[0], v1[1], v2[0], v2[1], v2[2], v3[0], v3[1], v3[2], v3[3], v3[4], v3[5]])
    low = plane_sends(*low[:2], *(after(v, v1) for v in swapped))
    vecs = four_sum(after(vecs, low[2], low[3]), "img", (2, 4, 6))
    high = plane_sums(*high, low[2], low[3])
    low = plane_sums(*low, vecs)
    parts, sent = owner_parts(low, high)
    given = lax.all_to_all(after(both, *sent), "band", 0, 0, tiled=True)
    block_out = given[:, 0].reshape(images.shape)
    input_grad = given[:, 1].reshape(images.shape).astype(F32)
    vecs = after(vecs, parts[1])
    vecs = vecs + lax.ppermute(vecs, "img", ACROSS_X)
    vector_grads = four_sum(vecs, "band", (1, 2, 3))
    vector_moments = MOMENTUM * vector_momentum + vector_grads
    vector_masters = vector_weight - LR_VECTOR * (vector_grads + MOMENTUM * vector_moments)
    vector_means = AVERAGE * vector_average + (1.0 - AVERAGE) * vector_masters
    matrix_grads = wide(*parts).reshape(-1)
    matrix_moments = MOMENTUM * matrix_momentum + matrix_grads
    matrix_masters = matrix_weight - LR_MATRIX * (matrix_grads + MOMENTUM * matrix_moments)
    matrix_means = AVERAGE * matrix_average + (1.0 - AVERAGE) * matrix_masters
    return (
        block_out,
        input_grad,
        matrix_grads,
        matrix_moments,
        matrix_means,
        matrix_masters,
        vector_grads,
        vector_moments,
        vector_means,
        vector_masters,
    )


def solution(mesh):
    fits = mesh.shape["img"] == 8 and mesh.shape["band"] == 4

    def per_device(images, *rest):
        step = whole_image if fits and images.shape[:3] == (4, 8, SIDE) else banded
        return step(images, *rest)

    return jax.shard_map(
            per_device,
        mesh=mesh,
        in_specs=(
            P("img", "band", None, None),
            P("img", "band", None, None),
            P("img"),
            P(("img", "band")),
            P(("img", "band")),
            P(("img", "band")),
            P(),
            P(),
            P(),
        ),
        out_specs=(
            P("img", "band", None, None),
            P("img", "band", None, None),
            P(("img", "band")),
            P(("img", "band")),
            P(("img", "band")),
            P(("img", "band")),
            P(),
            P(),
            P(),
            P(),
        ),
        check_vma=False,
    )
```

profile of v0, /device:TPU:0, one launch (start us, length us, event | category | flops | bytes accessed | tf_op | source)
XLA Modules:
  0.0 287.8 jit_solution(13391765995547133747)
XLA Ops:
  7.2 1.2 convert_element_type.221
  8.5 1.0 reshape.157
  9.5 21.2 %all_to_all.15 = bf16[4,256,512]{2,1,0:T(8,128)(2,1)} all-to-all(bf16[4,256,512]{2,1,0:T(8,128)(2,1)S(1)} %bitcast.122), channel_id=1, replica_groups=mesh['img'=8,'band'=4] {'band'}, dimensions={0} | all-to-all | bytes 2097152 | tf_op jit(solution)/shard_map/all_to_all | solution.py:997
  30.6 3.6 %all-to-all-start.1 = ((bf16[4,256,512]{2,1,0:T(8,128)(2,1)}), bf16[4,256,512]{2,1,0:T(8,128)(2,1)S(1)}, u32[]{:S(2)}, u32[]{:S(2)}) async-start(bf16[4,256,512]{2,1,0:T(8,128)(2,1)} %bitcast.5), calls=%async_computation.1 | async-start | bytes 2097152 | tf_op jit(solution)/shard_map/all_to_all | solution.py:997
  34.3 0.6 dynamic_slice.4
  34.9 1.3 pad_add_fusion.size_ref.at_ref
  36.2 4.2 %act_one.1 = (bf16[1088,512]{1,0:T(8,128)(2,1)}, bf16[512,1024]{1,0:T(8,128)(2,1)}, f32[8,512]{1,0:T(8,128)}) custom-call(s32[4]{0:T(128)} %pad_add_fusion.size_ref.at_ref, bf16[1024,512]{1,0:T(8,128)(2,1)} %bitcast.98, f32[11,512]{1,0:T(8,128)} %vec_ref.9), custom_call_target="tpu_custom_call" | custom-call | tf_op jit(solution)/shard_map/act_one/pallas_call | solution.py:336
  40.4 11.7 %all-to-all-done.1 = bf16[4,256,512]{2,1,0:T(8,128)(2,1)S(1)} async-done(((bf16[4,256,512]{2,1,0:T(8,128)(2,1)}), bf16[4,256,512]{2,1,0:T(8,128)(2,1)S(1)}, u32[]{:S(2)}, u32[]{:S(2)}) %all-to-all-start.1) | async-done | bytes 1048608 | tf_op jit(solution)/shard_map/all_to_all | solution.py:997
  52.0 55.6 %all-gather.2.cloned.1.call-done.w_any.k_any.k_ref = bf16[11264,512]{1,0:T(8,128)(2,1)} async-done(((bf16[352,512]{1,0:T(8,128)(2,1)}), bf16[11264,512]{1,0:T(8,128)(2,1)}) %all-gather.2.cloned.1.call-update) | async-done | bytes 11534352 | tf_op jit(solution)/shard_map/all_gather | solution.py:999
  107.6 43.9 %forward.1 = (f32[1024,512]{1,0:T(8,128)}, f32[8,512]{1,0:T(8,128)}, bf16[1024,512]{1,0:T(8,128)(2,1)}, f32[1024,512]{1,0:T(8,128)}, f32[1024,512]{1,0:T(8,128)}...) custom-call(s32[4]{0:T(128)} %pad_add_fusion.size_ref.at_ref, ...), custom_call_target="tpu_custom_call" | custom-call | tf_op jit(solution)/shard_map/forward/pallas_call | solution.py:336
  152.1 2.9 %collective-permute-done.1 = bf16[8,176,512]{2,1,0:T(8,128)(2,1)S(1)} collective-permute-done((bf16[8,176,512]{2,1,0:T(8,128)(2,1)}, bf16[8,176,512]{2,1,0:T(8,128)(2,1)S(1)}, u32[]{:S(2)}, u32[]{:S(2)}) %collective-permute-start.1) | collective-permute-done | bytes 1441824 | tf_op jit(solution)/shard_map/ppermute | solution.py:931
  155.1 1.8 fusion.refs_2_
  156.9 1.6 collective-permute-start.3
  158.7 0.9 copy-done.19
  159.6 0.5 collective-permute-start.2
  160.1 4.6 %block_rows.1.refs_3_.rows_ref = bf16[1024,512]{1,0:T(8,128)(2,1)} custom-call(s32[4]{0:T(128)} %pad_add_fusion.size_ref.at_ref, bf16[1024,512]{1,0:T(8,128)(2,1)} %get-tuple-element.42.mixed_ref, f32[1024,512]{1,0:T(8,128)} %get-tuple-element.43.resid_ref, f32[11,512]{1,0:T(8,128)} %vec_ref.9, bf16[11264,512]{1,0:T(8,128)(2,1)} %all-gather.2.cloned.1.call-done.w_any.k_any.k_ref), custom_call_target="tpu_custom_call" | custom-call | tf_op jit(solution)/shard_map/block_rows/pallas_call | solution.py:336
  164.8 18.8 %back_two.1 = (bf16[1088,1536]{1,0:T(8,128)(2,1)}, f32[8,512]{1,0:T(8,128)}, bf16[8,176,512]{2,1,0:T(8,128)(2,1)}, bf16[8,176,512]{2,1,0:T(8,128)(2,1)}, bf16[8,...) custom-call(s32[4]{0:T(128)} %pad_add_fusion.size_ref.at_ref, ...), custom_call_target="tpu_custom_call", output_to_operand_aliasing={{2}: (7, {}), {3}: (8, {}), {4}: (9, {}), {5}: (10, {})} | custom-call | tf_op jit(solution)/shard_map/back_two/pallas_call | solution.py:336
  183.7 0.8 copy-done
  184.8 0.5 collective-permute-start.4
  185.5 2.8 collective-permute-done.5
  188.3 2.2 fusion.1.refs_2_
  190.5 1.4 collective-permute-start.8
  191.9 2.2 add_convert_fusion.1
  194.1 0.6 collective-permute-start.6
  194.8 2.0 fusion.6
  196.7 1.4 collective-permute-start.13
  198.2 2.0 fusion.4
  200.1 0.6 collective-permute-start.14
  200.7 14.5 %back_one.1 = (bf16[4,2,256,512]{3,2,1,0:T(8,128)(2,1)}, f32[8,512]{1,0:T(8,128)}) custom-call(s32[4]{0:T(128)} %pad_add_fusion.size_ref.at_ref, bf16[1088,1536]{1,0:T(8,128)(2,1)} %after.16.e3_ref, bf16[11264,512]{1,0:T(8,128)(2,1)} %all-gather.2.cloned.1.call-done.w_any.k_any.k_ref, f32[11,512]{1,0:T(8,128)} %vec_ref.9, bf16[1024,512]{1,0:T(8,128)(2,1)} %bitcast.100, ...), custom_call_target="tpu_custom_call" | custom-call | tf_op jit(solution)/shard_map/back_one/pallas_call | solution.py:336
  215.2 0.7 slice.164
  215.9 0.6 pad_maximum_fusion.2.refs_0_
  216.6 2.1 fusion.9.refs_2_
  218.6 2.0 fusion.10.refs_1_
  220.6 1.7 collective-permute-start.10
  222.3 1.8 collective-permute-start.11
  224.1 1.4 collective-permute-start.7
  225.5 2.2 fusion.7
  227.7 0.7 collective-permute-start.12
  228.4 2.2 fusion.5
  230.7 0.6 add_add_fusion.1.refs_1_.refs_0_
  231.3 1.9 collective-permute-done.7.refs_0_
  233.2 2.2 fusion.11
  235.4 0.9 collective-permute-done.12.refs_0_
  236.3 0.7 copy-done.20
  237.0 1.6 fusion.8
  238.6 1.2 fusion.17
  239.8 1.3 fusion.16
  241.1 1.7 collective-permute-start.15
  242.9 0.8 collective-permute-start.16
  243.7 1.8 collective-permute-start.17
  245.5 3.6 %all-to-all-start.2 = ((bf16[4,2,256,512]{3,2,1,0:T(8,128)(2,1)}), bf16[4,2,256,512]{3,2,1,0:T(8,128)(2,1)S(1)}, u32[]{:S(2)}, u32[]{:S(2)}) async-start(bf16[4,2,256,512]{3,2,1,0:T(8,128)(2,1)} %after.24), calls=%async_computation.2 | async-start | bytes 4194304 | tf_op jit(solution)/shard_map/all_to_all | solution.py:1023
  249.1 5.8 %collective-permute-done.15.refs_1_ = bf16[352,512]{1,0:T(8,128)(2,1)} collective-permute-done((bf16[352,512]{1,0:T(8,128)(2,1)}, bf16[352,512]{1,0:T(8,128)(2,1)}, u32[]{:S(2)}, u32[]{:S(2)}) %collective-permute-start.15) | collective-permute-done | bytes 360480 | tf_op jit(solution)/shard_map/ppermute | solution.py:969
  254.9 0.8 collective-permute-start.18
  255.7 14.6 %collective-permute-done.16 = bf16[352,512]{1,0:T(8,128)(2,1)} collective-permute-done((bf16[352,512]{1,0:T(8,128)(2,1)}, bf16[352,512]{1,0:T(8,128)(2,1)}, u32[]{:S(2)}, u32[]{:S(2)}) %collective-permute-start.16) | collective-permute-done | bytes 360480 | tf_op jit(solution)/shard_map/ppermute | solution.py:969
  270.3 1.9 fusion.14
  272.5 0.5 copy-done.23
  273.0 0.9 collective-permute-start.20
  273.9 1.0 collective-permute-start.21
  274.9 1.5 multiply_add_fusion
  276.4 0.6 collective-permute-done.20
  277.1 0.4 collective-permute-done.21
  277.5 0.7 multiply_add_fusion.2
  278.1 1.2 fusion.20
  279.3 1.6 convert.17
  (99 shorter events, 1.6 us)
Async XLA Ops:
  7.2 2.3 copy-start.22
  7.2 100.4 %all-gather.2.cloned.1.call-start = ((), (), s32[]{:S(2)}) async-start(), calls=%async_computation.3 | async-start | bytes 11894784 | tf_op jit(solution)/shard_map/all_gather | solution.py:999
  30.6 3.7 %copy-start.31 = (s32[4]{0:T(128)S(1)}, s32[4]{0:T(128)}, u32[]{:S(2)}) copy-start(s32[4]{0:T(128)} %param.11) | copy-start | bytes 52
  30.6 21.4 %all-to-all-start.1 = ((bf16[4,256,512]{2,1,0:T(8,128)(2,1)}), bf16[4,256,512]{2,1,0:T(8,128)(2,1)S(1)}, u32[]{:S(2)}, u32[]{:S(2)}) async-start(bf16[4,256,512]{2,1,0:T(8,128)(2,1)} %bitcast.5), calls=%async_computation.1 | async-start | bytes 2097152 | tf_op jit(solution)/shard_map/all_to_all | solution.py:997
  52.0 55.6 %copy-start.9 = (bf16[4,256,512]{2,1,0:T(8,128)(2,1)}, bf16[4,256,512]{2,1,0:T(8,128)(2,1)S(1)}, u32[]{:S(2)}) copy-start(bf16[4,256,512]{2,1,0:T(8,128)(2,1)S(1)} %all-to-all-done.1) | copy-start | bytes 3145732
  151.6 6.9 %copy-start.18 = (bf16[8,176,512]{2,1,0:T(8,128)(2,1)S(1)}, bf16[8,176,512]{2,1,0:T(8,128)(2,1)}, u32[]{:S(2)}) copy-start(bf16[8,176,512]{2,1,0:T(8,128)(2,1)} %get-tuple-element.38) | copy-start | bytes 4325380
  151.6 3.5 %collective-permute-start.1 = (bf16[8,176,512]{2,1,0:T(8,128)(2,1)}, bf16[8,176,512]{2,1,0:T(8,128)(2,1)S(1)}, u32[]{:S(2)}, u32[]{:S(2)}) collective-permute-start(bf16[8,176,512]{2,1,0:T(8,128)(2,1)} %get-tuple-element.41), channel_id=1, source_target_pairs={{0,1},{1,0},{2,3},{3,2},{4,5},{5,4},{6,7},{7,6},{8,9},{9,8},{10,11... | collective-permute-start | bytes 4325384 | tf_op jit(solution)/shard_map/ppermute | solution.py:931
  151.9 6.6 %collective-permute-start = (bf16[8,176,512]{2,1,0:T(8,128)(2,1)}, bf16[8,176,512]{2,1,0:T(8,128)(2,1)S(1)}, u32[]{:S(2)}, u32[]{:S(2)}) collective-permute-start(bf16[8,176,512]{2,1,0:T(8,128)(2,1)} %get-tuple-element.39), channel_id=1, source_target_pairs={{0,1},{1,0},{2,3},{3,2},{4,5},{5,4},{6,7},{7,6},{8,9},{9,8},{10,11... | collective-permute-start | bytes 4325384 | tf_op jit(solution)/shard_map/ppermute | solution.py:931
  155.1 3.6 %copy-start.17 = (bf16[8,176,512]{2,1,0:T(8,128)(2,1)}, bf16[8,176,512]{2,1,0:T(8,128)(2,1)S(1)}, u32[]{:S(2)}) copy-start(bf16[8,176,512]{2,1,0:T(8,128)(2,1)S(1)} %collective-permute-done.1) | copy-start | bytes 4325380
  156.9 7.9 %copy-start.14 = (bf16[2,2,176,512]{3,2,1,0:T(8,128)(2,1)}, bf16[2,2,176,512]{3,2,1,0:T(8,128)(2,1)S(1)}, u32[]{:S(2)}) copy-start(bf16[2,2,176,512]{3,2,1,0:T(8,128)(2,1)S(1)} %fusion.refs_2_) | copy-start | bytes 2162692
  156.9 26.8 %collective-permute-start.3 = (bf16[2,2,176,512]{3,2,1,0:T(8,128)(2,1)S(1)}, bf16[2,2,176,512]{3,2,1,0:T(8,128)(2,1)S(1)}, u32[]{:S(2)}, u32[]{:S(2)}) collective-permute-start(bf16[2,2,176,512]{3,2,1,0:T(8,128)(2,1)S(1)} %fusion.refs_2_), channel_id=1, source_target_pairs={{0,2},{1,3},{2,0},{3,1},{4,6},{5,7},{6,4},{7,5},{8,10},{9,11},{10,... | collective-permute-start | bytes 2162696 | tf_op jit(solution)/shard_map/ppermute | solution.py:940
  158.5 1.1 copy-start.19
  158.7 6.1 %copy-start.15 = (bf16[4,176,512]{2,1,0:T(8,128)(2,1)}, bf16[4,176,512]{2,1,0:T(8,128)(2,1)S(1)}, u32[]{:S(2)}) copy-start(bf16[4,176,512]{2,1,0:T(8,128)(2,1)S(1)} %add_convert_fusion.3) | copy-start | bytes 2162692
  159.6 24.1 %collective-permute-start.2 = (bf16[2,2,176,512]{3,2,1,0:T(8,128)(2,1)S(1)}, bf16[2,2,176,512]{3,2,1,0:T(8,128)(2,1)S(1)}, u32[]{:S(2)}, u32[]{:S(2)}) collective-permute-start(bf16[2,2,176,512]{3,2,1,0:T(8,128)(2,1)S(1)} %bitcast.110), channel_id=1, source_target_pairs={{0,4},{4,0},{8,12},{12,8},{16,20},{20,16},{24,28},{28,24},{1,5},{5... | collective-permute-start | bytes 2162696 | tf_op jit(solution)/shard_map/ppermute | solution.py:940
  183.7 0.9 copy-start
  183.7 1.1 copy-start.2
  184.8 3.6 %collective-permute-start.5 = (bf16[8,176,512]{2,1,0:T(8,128)(2,1)}, bf16[8,176,512]{2,1,0:T(8,128)(2,1)}, u32[]{:S(2)}, u32[]{:S(2)}) collective-permute-start(bf16[8,176,512]{2,1,0:T(8,128)(2,1)} %after.15), channel_id=1, source_target_pairs={{0,1},{1,0},{2,3},{3,2},{4,5},{5,4},{6,7},{7,6},{8,9},{9,8},{10,11... | collective-permute-start | bytes 4325384 | tf_op jit(solution)/shard_map/ppermute | solution.py:931
  184.8 0.7 copy-start.30
  184.8 3.6 %copy-start.7 = (bf16[8,176,512]{2,1,0:T(8,128)(2,1)S(1)}, bf16[8,176,512]{2,1,0:T(8,128)(2,1)}, u32[]{:S(2)}) copy-start(bf16[8,176,512]{2,1,0:T(8,128)(2,1)} %get-tuple-element.54) | copy-start | bytes 4325380
  184.8 7.1 %copy-start.6 = (bf16[8,176,512]{2,1,0:T(8,128)(2,1)S(1)}, bf16[8,176,512]{2,1,0:T(8,128)(2,1)}, u32[]{:S(2)}) copy-start(bf16[8,176,512]{2,1,0:T(8,128)(2,1)} %get-tuple-element.52) | copy-start | bytes 4325380
  184.8 7.1 %collective-permute-start.4 = (bf16[8,176,512]{2,1,0:T(8,128)(2,1)}, bf16[8,176,512]{2,1,0:T(8,128)(2,1)}, u32[]{:S(2)}, u32[]{:S(2)}) collective-permute-start(bf16[8,176,512]{2,1,0:T(8,128)(2,1)} %after.14), channel_id=1, source_target_pairs={{0,1},{1,0},{2,3},{3,2},{4,5},{5,4},{6,7},{7,6},{8,9},{9,8},{10,11... | collective-permute-start | bytes 4325384 | tf_op jit(solution)/shard_map/ppermute | solution.py:931
  190.5 4.3 %copy-start.3 = (bf16[2,2,176,512]{3,2,1,0:T(8,128)(2,1)S(1)}, bf16[2,2,176,512]{3,2,1,0:T(8,128)(2,1)}, u32[]{:S(2)}) copy-start(bf16[2,2,176,512]{3,2,1,0:T(8,128)(2,1)} %copy-done.2) | copy-start | bytes 2162692
  190.5 26.1 %collective-permute-start.8 = (bf16[2,2,176,512]{3,2,1,0:T(8,128)(2,1)}, bf16[2,2,176,512]{3,2,1,0:T(8,128)(2,1)}, u32[]{:S(2)}, u32[]{:S(2)}) collective-permute-start(bf16[2,2,176,512]{3,2,1,0:T(8,128)(2,1)} %fusion.1.refs_2_), channel_id=1, source_target_pairs={{0,2},{1,3},{2,0},{3,1},{4,6},{5,7},{6,4},{7,5},{8,10},{9,11},{10,... | collective-permute-start | bytes 2162696 | tf_op jit(solution)/shard_map/ppermute | solution.py:940
  191.9 6.3 %copy-start.1 = (bf16[2,2,176,512]{3,2,1,0:T(8,128)(2,1)S(1)}, bf16[2,2,176,512]{3,2,1,0:T(8,128)(2,1)}, u32[]{:S(2)}) copy-start(bf16[2,2,176,512]{3,2,1,0:T(8,128)(2,1)} %copy-done) | copy-start | bytes 2162692
  194.1 24.5 %collective-permute-start.6 = (bf16[2,2,176,512]{3,2,1,0:T(8,128)(2,1)}, bf16[2,2,176,512]{3,2,1,0:T(8,128)(2,1)}, u32[]{:S(2)}, u32[]{:S(2)}) collective-permute-start(bf16[2,2,176,512]{3,2,1,0:T(8,128)(2,1)} %bitcast.11.refs_1_), channel_id=1, source_target_pairs={{0,4},{4,0},{8,12},{12,8},{16,20},{20,16},{24,28},{28,24},{1,5},{5... | collective-permute-start | bytes 2162696 | tf_op jit(solution)/shard_map/ppermute | solution.py:940
  196.7 27.4 %collective-permute-start.13 = (bf16[2,176,512]{2,1,0:T(8,128)(2,1)}, bf16[2,176,512]{2,1,0:T(8,128)(2,1)}, u32[]{:S(2)}, u32[]{:S(2)}) collective-permute-start(bf16[2,176,512]{2,1,0:T(8,128)(2,1)} %fusion.6), channel_id=1, source_target_pairs={{0,2},{1,3},{2,0},{3,1},{4,6},{5,7},{6,4},{7,5},{8,10},{9,11},{10,... | collective-permute-start | bytes 1081352 | tf_op jit(solution)/shard_map/ppermute | solution.py:952
  200.1 27.6 %collective-permute-start.14 = (bf16[2,176,512]{2,1,0:T(8,128)(2,1)}, bf16[2,176,512]{2,1,0:T(8,128)(2,1)}, u32[]{:S(2)}, u32[]{:S(2)}) collective-permute-start(bf16[2,176,512]{2,1,0:T(8,128)(2,1)} %fusion.4), channel_id=1, source_target_pairs={{0,4},{4,0},{8,12},{12,8},{16,20},{20,16},{24,28},{28,24},{1,5},{5... | collective-permute-start | bytes 1081352 | tf_op jit(solution)/shard_map/ppermute | solution.py:953
  200.7 15.2 %copy-start.29 = (f32[8,512]{1,0:T(8,128)S(1)}, f32[8,512]{1,0:T(8,128)}, u32[]{:S(2)}) copy-start(f32[8,512]{1,0:T(8,128)} %get-tuple-element.61) | copy-start | bytes 49156
  220.6 7.1 %copy-start.8 = (bf16[2,176,512]{2,1,0:T(8,128)(2,1)S(1)}, bf16[2,176,512]{2,1,0:T(8,128)(2,1)}, u32[]{:S(2)}) copy-start(bf16[2,176,512]{2,1,0:T(8,128)(2,1)} %fusion.9.refs_2_) | copy-start | bytes 1081348
  220.6 10.1 %collective-permute-start.10 = (f32[11,512]{1,0:T(8,128)}, f32[11,512]{1,0:T(8,128)S(1)}, u32[]{:S(2)}, u32[]{:S(2)}) collective-permute-start(f32[11,512]{1,0:T(8,128)} %after.19), channel_id=1, source_target_pairs={{0,16},{4,20},{8,24},{12,28},{16,0},{20,4},{24,8},{28,12},{1,17},{... | collective-permute-start | bytes 67592 | tf_op jit(solution)/shard_map/ppermute | solution.py:974
  222.3 8.4 %collective-permute-start.11 = (f32[11,512]{1,0:T(8,128)}, f32[11,512]{1,0:T(8,128)S(1)}, u32[]{:S(2)}, u32[]{:S(2)}) collective-permute-start(f32[11,512]{1,0:T(8,128)} %after.19), channel_id=1, source_target_pairs={{0,24},{4,28},{8,16},{12,20},{16,8},{20,12},{24,0},{28,4},{1,25},{... | collective-permute-start | bytes 67592 | tf_op jit(solution)/shard_map/ppermute | solution.py:974
  224.1 6.6 %collective-permute-start.9 = (f32[11,512]{1,0:T(8,128)}, f32[11,512]{1,0:T(8,128)S(1)}, u32[]{:S(2)}, u32[]{:S(2)}) collective-permute-start(f32[11,512]{1,0:T(8,128)} %after.19), channel_id=1, source_target_pairs={{0,8},{4,12},{8,0},{12,4},{16,24},{20,28},{24,16},{28,20},{1,9},{5... | collective-permute-start | bytes 67592 | tf_op jit(solution)/shard_map/ppermute | solution.py:974
  224.1 9.1 %collective-permute-start.7 = (bf16[2,176,512]{2,1,0:T(8,128)(2,1)}, bf16[2,176,512]{2,1,0:T(8,128)(2,1)}, u32[]{:S(2)}, u32[]{:S(2)}) collective-permute-start(bf16[2,176,512]{2,1,0:T(8,128)(2,1)} %fusion.10.refs_1_), channel_id=1, source_target_pairs={{0,2},{1,3},{2,0},{3,1},{4,6},{5,7},{6,4},{7,5},{8,10},{9,11},{10,... | collective-permute-start | bytes 1081352 | tf_op jit(solution)/shard_map/ppermute | solution.py:952
  227.7 2.9 %copy-start.26 = (f32[11,512]{1,0:T(8,128)S(1)}, f32[11,512]{1,0:T(8,128)}, u32[]{:S(2)}) copy-start(f32[11,512]{1,0:T(8,128)} %after.19) | copy-start | bytes 67588
  227.7 8.6 %collective-permute-start.12 = (bf16[2,176,512]{2,1,0:T(8,128)(2,1)S(1)}, bf16[2,176,512]{2,1,0:T(8,128)(2,1)S(1)}, u32[]{:S(2)}, u32[]{:S(2)}) collective-permute-start(bf16[2,176,512]{2,1,0:T(8,128)(2,1)S(1)} %copy-done.8), channel_id=1, source_target_pairs={{0,4},{4,0},{8,12},{12,8},{16,20},{20,16},{24,28},{28,24},{1,5},{5... | collective-permute-start | bytes 1081352 | tf_op jit(solution)/shard_map/ppermute | solution.py:953
  235.4 3.2 %copy-start.12 = (f32[2,176,512]{2,1,0:T(8,128)S(1)}, f32[2,176,512]{2,1,0:T(8,128)}, u32[]{:S(2)}) copy-start(f32[2,176,512]{2,1,0:T(8,128)} %fusion.7) | copy-start | bytes 2162692
  235.4 3.2 %copy-start.13 = (f32[2,176,512]{2,1,0:T(8,128)S(1)}, f32[2,176,512]{2,1,0:T(8,128)}, u32[]{:S(2)}) copy-start(f32[2,176,512]{2,1,0:T(8,128)} %fusion.5) | copy-start | bytes 2162692
  236.3 0.7 copy-start.20
  237.0 1.6 copy-start.16
  239.8 1.3 copy-start.4
  239.8 1.3 copy-start.5
  241.1 13.8 %collective-permute-start.15 = (bf16[352,512]{1,0:T(8,128)(2,1)}, bf16[352,512]{1,0:T(8,128)(2,1)}, u32[]{:S(2)}, u32[]{:S(2)}) collective-permute-start(bf16[352,512]{1,0:T(8,128)(2,1)} %get-tuple-element.75.refs_1_), channel_id=1, source_target_pairs={{0,8},{4,12},{8,0},{12,4},{16,24},{20,28},{24,16},{28,20},{1,9},{5... | collective-permute-start | bytes 1081352 | tf_op jit(solution)/shard_map/ppermute | solution.py:969
  242.9 27.4 %collective-permute-start.16 = (bf16[352,512]{1,0:T(8,128)(2,1)}, bf16[352,512]{1,0:T(8,128)(2,1)}, u32[]{:S(2)}, u32[]{:S(2)}) collective-permute-start(bf16[352,512]{1,0:T(8,128)(2,1)} %get-tuple-element.74.refs_2_), channel_id=1, source_target_pairs={{0,16},{4,20},{8,24},{12,28},{16,0},{20,4},{24,8},{28,12},{1,17},{... | collective-permute-start | bytes 1081352 | tf_op jit(solution)/shard_map/ppermute | solution.py:969
  243.7 26.6 %collective-permute-start.17 = (bf16[352,512]{1,0:T(8,128)(2,1)}, bf16[352,512]{1,0:T(8,128)(2,1)}, u32[]{:S(2)}, u32[]{:S(2)}) collective-permute-start(bf16[352,512]{1,0:T(8,128)(2,1)} %get-tuple-element.69.refs_3_), channel_id=1, source_target_pairs={{0,24},{4,28},{8,16},{12,20},{16,8},{20,12},{24,0},{28,4},{1,25},{... | collective-permute-start | bytes 1081352 | tf_op jit(solution)/shard_map/ppermute | solution.py:969
  245.5 32.6 %all-to-all-start.2 = ((bf16[4,2,256,512]{3,2,1,0:T(8,128)(2,1)}), bf16[4,2,256,512]{3,2,1,0:T(8,128)(2,1)S(1)}, u32[]{:S(2)}, u32[]{:S(2)}) async-start(bf16[4,2,256,512]{3,2,1,0:T(8,128)(2,1)} %after.24), calls=%async_computation.2 | async-start | bytes 4194304 | tf_op jit(solution)/shard_map/all_to_all | solution.py:1023
  254.9 17.6 %collective-permute-start.18 = (f32[11,512]{1,0:T(8,128)}, f32[11,512]{1,0:T(8,128)S(1)}, u32[]{:S(2)}, u32[]{:S(2)}) collective-permute-start(f32[11,512]{1,0:T(8,128)} %after.25), channel_id=1, source_target_pairs={{0,4},{4,0},{8,12},{12,8},{16,20},{20,16},{24,28},{28,24},{1,5},{5... | collective-permute-start | bytes 67592 | tf_op jit(solution)/shard_map/ppermute | solution.py:1027
  270.3 4.6 %copy-start.25 = (f32[180224]{0:T(1024)S(1)}, f32[180224]{0:T(1024)}, u32[]{:S(2)}) copy-start(f32[180224]{0:T(1024)} %param.13) | copy-start | bytes 2162692
  272.2 0.8 copy-start.23
  272.2 2.6 copy-start.10
  272.3 2.6 copy-start.24
  272.5 4.0 %copy-start.11 = (f32[44,4,8,128]{3,1,2,0:T(4,128)}, f32[44,4,8,128]{3,1,2,0:T(4,128)S(1)}, u32[]{:S(2)}) copy-start(f32[44,4,8,128]{3,1,2,0:T(4,128)S(1)} %copy.36) | copy-start | bytes 2162692
  273.0 3.4 %collective-permute-start.19 = (f32[11,512]{1,0:T(8,128)S(1)}, f32[11,512]{1,0:T(8,128)S(1)}, u32[]{:S(2)}, u32[]{:S(2)}) collective-permute-start(f32[11,512]{1,0:T(8,128)S(1)} %add.205), channel_id=1, source_target_pairs={{0,1},{1,0},{2,3},{3,2},{4,5},{5,4},{6,7},{7,6},{8,9},{9,8},{10,11... | collective-permute-start | bytes 67592 | tf_op jit(solution)/shard_map/ppermute | solution.py:974
  273.0 4.1 %collective-permute-start.20 = (f32[11,512]{1,0:T(8,128)S(1)}, f32[11,512]{1,0:T(8,128)S(1)}, u32[]{:S(2)}, u32[]{:S(2)}) collective-permute-start(f32[11,512]{1,0:T(8,128)S(1)} %add.205), channel_id=1, source_target_pairs={{0,2},{1,3},{2,0},{3,1},{4,6},{5,7},{6,4},{7,5},{8,10},{9,11},{10,... | collective-permute-start | bytes 67592 | tf_op jit(solution)/shard_map/ppermute | solution.py:974
  273.9 3.6 %collective-permute-start.21 = (f32[11,512]{1,0:T(8,128)S(1)}, f32[11,512]{1,0:T(8,128)S(1)}, u32[]{:S(2)}, u32[]{:S(2)}) collective-permute-start(f32[11,512]{1,0:T(8,128)S(1)} %add.205), channel_id=1, source_target_pairs={{0,3},{1,2},{2,1},{3,0},{4,7},{5,6},{6,5},{7,4},{8,11},{9,10},{10,... | collective-permute-start | bytes 67592 | tf_op jit(solution)/shard_map/ppermute | solution.py:974
  274.9 2.6 copy-start.21
  274.9 2.6 copy-start.27
  274.9 2.6 copy-start.28
Sparse Core Ops, SparseCore 0:
  11.4 96.1 all-gather.1
where the time goes:
time: 290 us; the launch traced here: 288 us
  waiting for transfers between devices  97.2 us (34%)
  Pallas kernels  86.1 us (30%)
  other arithmetic  34.5 us (12%)
  starting transfers between devices  27.1 us (9%)
  blocking collectives  21.2 us (7%)
  between operations  14.4 us (5%)
  local copies, waits for them, and re-layouts  7.21 us (2%)
    pallas_call x5, Pallas kernels, call(): pl.pallas_call(body, out_shape=[o for o, _ in outs], in_specs=[spaces[s]...  86.1 us
    all_gather x1, waiting for transfers between devices, whole_image(): lax.all_gather(matrix_weight.astype(BF16).reshape(-1, c), ALL, axis=0, ti...  55.6 us
    all_to_all x1, blocking collectives, to_image(): return lax.all_to_all(parts, 'band', 0, 0, tiled=True).reshape(n, c)  21.2 us
    ppermute x3, waiting for transfers between devices, owner_parts(): lax.ppermute(v, 'img', [(i, i ^ 2 * step) for i in range(8)])  20.4 us
    all_to_all x1, waiting for transfers between devices, to_image(): return lax.all_to_all(parts, 'band', 0, 0, tiled=True).reshape(n, c)  11.7 us
    add x4, other arithmetic, wide(): total = total + part.astype(F32)  8.25 us
  transfers between devices with their start and end apart: 25, of which 10 were waited for; matrix products, arithmetic and copies ran while one was open for 10% of the time, Pallas kernels for 15%

commit v1 on v0

--- a/solution.py
+++ b/solution.py
@@ -472,16 +472,41 @@
 COLUMNS = (1, 0, 2)
 
 
-def start_kernel(src_ref, dst_ref, sems, offset):
+def fetch_rows(at_ref, gathered, dst_ref, base, row, count, sem):
+    heads, mine, other = gathered
+    tail = mine.shape[1]
+    head = heads.shape[0] // 32
+    block = head + tail
+    for owner in range(row // block, (row + count - 1) // block + 1):
+        first = owner * block
+        lo, hi = max(row, first), min(row + count, first + head)
+        if lo < hi:
+            inside = pl.ds(base + lo - row, hi - lo)
+            pltpu.make_async_copy(heads.at[pl.ds(owner * head + lo - first, hi - lo)], dst_ref.at[inside], sem).start()
+        lo, hi = max(row, first + head), min(row + count, first + block)
+        if lo >= hi:
+            continue
+        inside = pl.ds(base + lo - row, hi - lo)
+        z, x, y, c = at_ref[4] ^ (owner >> 3), at_ref[1] ^ ((owner >> 2) & 1), at_ref[2] ^ ((owner >> 1) & 1), owner & 1
+        slot = jnp.where(z < 2, x * 4 + y * 2 + z, 6 + y * 4 + x * 2 + z)
+        place = pl.ds(lo - first - head, hi - lo)
+        for far, ref in enumerate((mine, other)):
+
+            @pl.when((at_ref[3] ^ c) == far)
+            def _(ref=ref, place=place, inside=inside, slot=slot):
+                pltpu.make_async_copy(ref.at[slot, place], dst_ref.at[inside], sem).start()
+
+    whole = dst_ref.at[pl.ds(base, count)]
+    return pltpu.make_async_copy(whole, whole, sem)
+
+
+def start_kernel(at_ref, gathered, dst_ref, sems, row):
     c = dst_ref.shape[1]
     copies = {}
     for dx in COLUMNS:
         for dy in range(3):
             tap = 3 * dy + dx
-            copies[tap] = pltpu.make_async_copy(
-                src_ref.at[pl.ds(offset + tap * c, c)], dst_ref.at[pl.ds(tap * c, c)], sems.at[tap]
-            )
-            copies[tap].start()
+            copies[tap] = fetch_rows(at_ref, gathered, dst_ref, tap * c, row + tap * c, c, sems.at[tap])
     return copies
 
 
@@ -556,8 +581,8 @@
 
 
 def forward_body(
-    at_ref, pad_one_ref, vec_ref, w_any, img_any, cot_any,
-    conv_any, stat_two_ref, mixed_any, resid_any, grad_any, e3_any, vout_ref, *refs,
+    at_ref, pad_one_ref, vec_ref, heads_any, mine_any, other_any, img_any, cot_any,
+    weights_any, conv_any, stat_two_ref, mixed_any, resid_any, grad_any, e3_any, vout_ref, *refs,
 ):
     high, low = refs[0:4], refs[4:8]
     (k_one, k_two, w_ref, img_ref, cot_ref, conv_ref, pad_ref, act_t, resid_ref, normed_ref, normed_t,
@@ -565,12 +590,13 @@
      one_sems, two_sems, w_sems, in_sems, out_sems, gw_sem, gk_sems) = refs[8:]
     n, c = normed_ref.shape
     size = at_ref[0]
-    one_copies = start_kernel(w_any, k_one, one_sems, 0)
-    two_copies = start_kernel(w_any, k_two, two_sems, 9 * c)
+    gathered = (heads_any, mine_any, other_any)
+    one_copies = start_kernel(at_ref, gathered, k_one, one_sems, 0)
     img_copy = pltpu.make_async_copy(img_any, img_ref, in_sems.at[0])
     cot_copy = pltpu.make_async_copy(cot_any, cot_ref, in_sems.at[1])
     img_copy.start()
-    w_copies = start_copies(w_any, w_ref, w_sems, 4, 18 * c)
+    two_copies = start_kernel(at_ref, gathered, k_two, two_sems, 9 * c)
+    w_copies = [fetch_rows(at_ref, gathered, w_ref, j * c, (18 + j) * c, c, w_sems.at[j]) for j in range(4)]
     cot_copy.start()
     leaving = []
 
@@ -591,6 +617,8 @@
 
     s1, s2 = conv(pad_one_ref, k_one, one_copies, conv_ref, MB, finish_one)
     leave(conv_ref, conv_any)
+    leave(k_one, weights_any.at[pl.ds(0, 9 * c)])
+    kept_one = leaving[-1]
     mean, scale = moments(s1, s2, size)
     put_stats(stat_two_ref, mean, scale)
     apply_norm(conv_ref, mean, scale * vec_ref[3:4, :], vec_ref[4:5, :], mask, pad_ref)
@@ -606,6 +634,7 @@
 
     s1, s2 = conv(pad_ref, k_two, two_copies, resid_ref, MB, finish_two)
     leave(resid_ref, resid_any)
+    leave(k_two, weights_any.at[pl.ds(9 * c, 9 * c)])
     mean, scale = moments(s1, s2, size)
     gain = vec_ref[6:7, :]
     full_gain, shift = scale * gain, vec_ref[7:8, :]
@@ -623,6 +652,7 @@
 
     for copy in w_copies:
         copy.wait()
+    leave(w_ref, weights_any.at[pl.ds(18 * c, 4 * c)])
     factor = c ** (-0.5)
     wq, wk, wv, wo = (functools.partial(lambda j: w_ref[j * c : (j + 1) * c, :], j) for j in range(4))
     qb, vb = vec_ref[8:9, :], vec_ref[9:10, :]
@@ -700,48 +730,33 @@
     leave(e3_ref, e3_any)
     leave(grad_ref, grad_any)
     vout_ref[...] = total_of(sg, sux, su, sq, sv, top_sum)
+    still = [v for v in leaving if v is not kept_one]
+    kept_one.wait()
     waits += kernel_gradient(act_t, e3_ref, k_one, 9 * c, at_ref, (low, high), gk_sems)
-    for wait in waits + leaving:
+    for wait in waits + still:
         wait.wait()
 
 
-def forward(at, pad_one, vec, weights, img, cot):
+def forward(at, pad_one, vec, gathered, img, cot):
     n, c = img.shape
-    half = (shape((8, weights.shape[0] // 64, c), BF16), "a")
+    heads, mine, other = gathered
+    half = (shape((8, 22 * c // 64, c), BF16), "a")
 
     def low(*dims):
         return pltpu.VMEM(dims, BF16)
 
     full = low(n, c)
     found = call(forward_body,
-        [(shape((n, c), F32), "a"), (shape((8, c), F32), "v"), (shape((n, c), BF16), "a"), (shape((n, c), F32), "a"),
+        [(shape((22 * c, c), BF16), "a"), (shape((n, c), F32), "a"), (shape((8, c), F32), "v"), (shape((n, c), BF16), "a"), (shape((n, c), F32), "a"),
          (shape((n, c), F32), "a"), (shape((n + 2 * SIDE, 3 * c), BF16), "a"), (shape((8, c), F32), "v")] + [half] * 8,
-        [(at, "s"), (pad_one, "v"), (vec, "v"), (weights, "a"), (img, "a"), (cot, "a")],
+        [(at, "s"), (pad_one, "v"), (vec, "v"), (heads, "a"), (mine, "a"), (other, "a"), (img, "a"), (cot, "a")],
         [low(9 * c, c), low(9 * c, c), low(4 * c, c), full, full, pltpu.VMEM((n, c), F32), low(n + 2 * SIDE, c), low(c, n),
          pltpu.VMEM((n, c), F32), full, low(c, n), full, full, full, low(n, n), low(n, n), full, full, full, full, full, full,
          pltpu.VMEM((n, c), F32), low(n + 2 * SIDE, 3 * c), low(4 * c, c),
          pltpu.SemaphoreType.DMA((9,)), pltpu.SemaphoreType.DMA((9,)), pltpu.SemaphoreType.DMA((4,)),
-         pltpu.SemaphoreType.DMA((2,)), pltpu.SemaphoreType.DMA((5,)), pltpu.SemaphoreType.DMA, pltpu.SemaphoreType.DMA((9,))],
+         pltpu.SemaphoreType.DMA((2,)), pltpu.SemaphoreType.DMA((8,)), pltpu.SemaphoreType.DMA, pltpu.SemaphoreType.DMA((9,))],
         name="forward")
-    return found[:7], found[7:11], found[11:15]
-
-
-def out_body(at_ref, mixed_ref, resid_ref, vec_ref, w_any, out_ref, wo_ref, sem):
-    n, c = mixed_ref.shape
-    copy = pltpu.make_async_copy(w_any.at[pl.ds(21 * c, c)], wo_ref, sem)
-    copy.start()
-    copy.wait()
-    for m in range(n // MB):
-        at = slice(m * MB, (m + 1) * MB)
-        value = dot(mixed_ref[at, :], wo_ref[...]) + vec_ref[10:11, :] + resid_ref[at, :]
-        out_ref[at, :] = jnp.where(pixel_mask(at_ref[0], m * MB, MB, c), value, 0.0).astype(BF16)
-
-
-def block_rows(at, mixed, resid, vec, weights):
-    n, c = mixed.shape
-    return call(out_body, [(shape((n, c), BF16), "v")],
-        [(at, "s"), (mixed, "v"), (resid, "v"), (vec, "v"), (weights, "a")],
-        [pltpu.VMEM((c, c), BF16), pltpu.SemaphoreType.DMA], name="block_rows")[0]
+    return found[:8], found[8:12], found[12:16]
 
 
 def kernel_gradient(act_t, e3_ref, stage, row, at_ref, rounds, sems):
@@ -853,44 +868,65 @@
 
 
 def back_one_body(
-    size_ref, e3_ref, k_ref, vec_ref, img_ref, stat_ref, resid_ref, rows_ref, both_any, vout_ref,
-    g_ref, out_ref, k_vmem, sems, rows_sem, out_sem,
+    size_ref, e3_ref, k_ref, vec_ref, img_ref, stat_ref, grad_ref, mixed_any, resid_any, both_any, vout_ref,
+    g_ref, out_ref, rows_ref, mixed_ref, resid_ref, wo_ref, k_vmem, sems, in_sems, out_sems,
 ):
     n, c = img_ref.shape
     copies = start_copies(k_ref, k_vmem, sems, 3)
     bands, quarter = both_any.shape[0], both_any.shape[2]
-    kept = [pltpu.make_async_copy(rows_ref.at[pl.ds(j * quarter, quarter)], both_any.at[j, 0], rows_sem.at[j]) for j in range(bands)]
-    for copy in kept:
+    later = [
+        pltpu.make_async_copy(src, dst, in_sems.at[i])
+        for i, (src, dst) in enumerate(((mixed_any, mixed_ref), (resid_any, resid_ref), (k_ref.at[pl.ds(21 * c, c)], wo_ref)))
+    ]
+    for copy in later:
         copy.start()
+    leaving = []
+
+    def leave(src_ref, which):
+        for j in range(bands):
+            copy = pltpu.make_async_copy(src_ref.at[pl.ds(j * quarter, quarter)], both_any.at[j, which], out_sems.at[len(leaving)])
+            copy.start()
+            leaving.append(copy)
+
     size = size_ref[0]
     mask = row_mask(size, c)
     conv_back(e3_ref, k_vmem, copies, g_ref)
+    for copy in later:
+        copy.wait()
+
+    def block_rows(m, carry):
+        first = pl.multiple_of(m * MB, MB)
+        at = pl.ds(first, MB)
+        value = dot(mixed_ref[at, :], wo_ref[...]) + vec_ref[10:11, :] + resid_ref[at, :]
+        rows_ref[at, :] = jnp.where(pixel_mask(size, first, MB, c), value, 0.0).astype(BF16)
+        return carry
+
+    lax.fori_loop(0, n // MB, block_rows, 0)
+    leave(rows_ref, 0)
     mean, scale = stat_ref[0:1, :], stat_ref[1:2, :]
     gain, shift = vec_ref[0:1, :], vec_ref[1:2, :]
     su, sux, m1, m2 = norm_back_sums(img_ref, g_ref, mean, scale, gain, shift, mask, size)
 
     def apply(h, carry):
         xhat = (img_ref[rows(h), :].astype(F32) - mean) * scale
-        g = (g_ref[rows(h), :] * gain - m1 - xhat * m2) * scale + resid_ref[rows(h), :]
+        g = (g_ref[rows(h), :] * gain - m1 - xhat * m2) * scale + grad_ref[rows(h), :]
         out_ref[rows(h), :] = jnp.where(mask(h), g, 0.0).astype(out_ref.dtype)
         return carry
 
     lax.fori_loop(0, SIDE, apply, 0, unroll=2)
-    for j in range(bands):
-        copy = pltpu.make_async_copy(out_ref.at[pl.ds(j * quarter, quarter)], both_any.at[j, 1], out_sem.at[j])
-        copy.start()
-        kept.append(copy)
+    leave(out_ref, 1)
     vout_ref[...] = total_of(sux, su)
-    for copy in kept:
+    for copy in leaving:
         copy.wait()
 
 
-def back_one(at, e3, weights, vec, img, stat, grad_resid, out, bands):
+def back_one(at, e3, weights, vec, img, stat, grad_resid, mixed, resid, bands):
     n, c = img.shape
+    low, full = pltpu.VMEM((n, c), BF16), pltpu.VMEM((n, c), F32)
     return call(back_one_body, [(shape((bands, 2, n // bands, c), BF16), "a"), (shape((8, c), F32), "v")],
-        [(at, "s"), (e3, "v"), (weights, "a"), (vec, "v"), (img, "v"), (stat, "v"), (grad_resid, "v"), (out, "v")],
-        [pltpu.VMEM((n, c), F32), pltpu.VMEM((n, c), BF16), pltpu.VMEM((9 * c, c), BF16), pltpu.SemaphoreType.DMA((3,)),
-         pltpu.SemaphoreType.DMA((bands,)), pltpu.SemaphoreType.DMA((bands,))],
+        [(at, "s"), (e3, "v"), (weights, "a"), (vec, "v"), (img, "v"), (stat, "v"), (grad_resid, "v"), (mixed, "a"), (resid, "a")],
+        [full, low, low, low, full, pltpu.VMEM((c, c), BF16), pltpu.VMEM((9 * c, c), BF16), pltpu.SemaphoreType.DMA((3,)),
+         pltpu.SemaphoreType.DMA((3,)), pltpu.SemaphoreType.DMA((2 * bands,))],
         name="back_one")
 
 
@@ -946,6 +982,15 @@
     kept_a = (*(v[0, 0] for v in pair_a), got_a[0])
     kept_b = (*(v[0, 0] for v in pair_b), got_b[0])
     return kept_a, kept_b, next_a, next_b
+
+
+def plane_gather(own):
+    z = [lax.ppermute(own, "img", [(i, i ^ (2 * step)) for i in range(8)]) for step in (1, 2, 3)]
+    first, last = jnp.stack([own, z[0]]), jnp.stack([z[1], z[2]])
+    first = jnp.concatenate([first, lax.ppermute(first, "band", ACROSS_Y)])
+    last = jnp.concatenate([last, lax.ppermute(last, "img", ACROSS_X)])
+    mine = jnp.concatenate([first, lax.ppermute(first, "img", ACROSS_X), last, lax.ppermute(last, "band", ACROSS_Y)])
+    return mine, lax.ppermute(mine, "band", CORE)
 
 
 def plane_sums(kept_a, kept_b, next_a, next_b, *earlier):
@@ -990,22 +1035,23 @@
     n = width * width
     mine = lax.axis_index("band")
     place = lax.axis_index("img")
-    at = jnp.stack([lax.dynamic_index_in_dim(sizes, mine, 0, False), place % 2, mine // 2, mine % 2])
+    at = jnp.stack([lax.dynamic_index_in_dim(sizes, mine, 0, False), place % 2, mine // 2, mine % 2, place // 2])
 
     def to_image(field):
         parts = field.reshape(batch, height * width, c)
         return lax.all_to_all(parts, "band", 0, 0, tiled=True).reshape(n, c)
 
-    weights = lax.all_gather(matrix_weight.astype(BF16).reshape(-1, c), ALL, axis=0, tiled=True)
+    own = matrix_weight.astype(BF16).reshape(-1, c)
+    head = 288
+    gathered = (lax.all_gather(own[:head], ALL, axis=0, tiled=True), *plane_gather(own[head:]))
     img = to_image(images)
     cot = to_image(cotangent)
     pad_one, act_t, stat_one = act_one(at, img, vector_weight)
-    (conv_out, stat_two, mixed, resid, grad_resid, e3_two, v3), high, low = forward(
-        at, pad_one, vector_weight, weights, img, cot
+    (weights, conv_out, stat_two, mixed, resid, grad_resid, e3_two, v3), high, low = forward(
+        at, pad_one, vector_weight, gathered, img, cot
     )
     high = chip_sends(high)
-    out = block_rows(at, mixed, resid, vector_weight, weights)
-    e3_two = after(e3_two, high[2], high[3], out)
+    e3_two = after(e3_two, high[2], high[3])
     swapped = plane_swap(high[2], high[3])
     e3_one, v2, low = back_two(at, e3_two, weights, vector_weight, conv_out, stat_two, act_t, low)
     low = chip_sends(low, *swapped)
@@ -1013,7 +1059,7 @@
     low_sends = low[2:4]
     e3_one = after(e3_one, *low_sends)
     swapped = plane_swap(low[2], low[3])
-    both, v1 = back_one(at, e3_one, weights, vector_weight, img, stat_one, grad_resid, out, batch)
+    both, v1 = back_one(at, e3_one, weights, vector_weight, img, stat_one, grad_resid, mixed, resid, batch)
     vecs = jnp.stack([v1[0], v1[1], v2[0], v2[1], v2[2], v3[0], v3[1], v3[2], v3[3], v3[4], v3[5]])
     low = plane_sends(*low[:2], *(after(v, v1) for v in swapped))
     vecs = four_sum(after(vecs, low[2], low[3]), "img", (2, 4, 6))

time: 290 us -> 278 us (0.959)
  blocking collectives: 21.2 us -> 0 us
  starting transfers between devices: 27.1 us -> 44.5 us
  waiting for transfers between devices: 97.2 us -> 92.2 us
  Pallas kernels: 86.1 us -> 82.3 us
    all_gather x1, waiting for transfers between devices: 55.6 us -> 28.4 us  [whole_image(): lax.all_gather(own[:head], ALL, axis=0, tiled=True)]
    ppermute x0 -> x8, waiting for transfers between devices: none -> 27.1 us  [the longest x1 15.2 us: plane_gather(): first = jnp.concatenate([first, lax.ppermute(first, 'band', ACROSS_Y)])]
    all_to_all x1 -> x0, blocking collectives: 21.2 us -> none  [to_image(): return lax.all_to_all(parts, 'band', 0, 0, tiled=True).reshape(n, c)]
    ppermute x0 -> x8, starting transfers between devices: none -> 11.6 us  [the longest x3 5.68 us: plane_gather(): lax.ppermute(own, 'img', [(i, i ^ 2 * step) for i in range(8)])]
    pallas_call x5 -> x4, Pallas kernels: 86.1 us -> 82.3 us  [call(): pl.pallas_call(body, out_shape=[o for o, _ in outs], in_specs=[spaces[s]...]
    all_to_all x1 -> x2, starting transfers between devices: 3.65 us -> 7.05 us  [to_image(): return lax.all_to_all(parts, 'band', 0, 0, tiled=True).reshape(n, c)]
    all_to_all x1 -> x2, waiting for transfers between devices: 11.7 us -> 9.34 us  [to_image(): return lax.all_to_all(parts, 'band', 0, 0, tiled=True).reshape(n, c)]
  transfers between devices with their start and end apart: 25 -> 34, of which waited for: 10 -> 14; matrix products, arithmetic and copies ran while one was open for 10% -> 11% of each run, Pallas kernels for 15% -> 14%
where the time goes in v1:
time: 278 us; the launch traced here: 275 us
  waiting for transfers between devices  92.2 us (33%)
  Pallas kernels  82.3 us (30%)
  starting transfers between devices  44.5 us (16%)
  other arithmetic  33.6 us (12%)
  between operations  14.5 us (5%)
  local copies, waits for them, and re-layouts  7.92 us (3%)
    pallas_call x4, Pallas kernels, call(): pl.pallas_call(body, out_shape=[o for o, _ in outs], in_specs=[spaces[s]...  82.3 us
    all_gather x1, waiting for transfers between devices, whole_image(): lax.all_gather(own[:head], ALL, axis=0, tiled=True)  28.4 us
    ppermute x3, waiting for transfers between devices, owner_parts(): lax.ppermute(v, 'img', [(i, i ^ 2 * step) for i in range(8)])  18.3 us
    ppermute x1, waiting for transfers between devices, plane_gather(): first = jnp.concatenate([first, lax.ppermute(first, 'band', ACROSS_Y)])  15.2 us
    all_to_all x2, waiting for transfers between devices, to_image(): return lax.all_to_all(parts, 'band', 0, 0, tiled=True).reshape(n, c)  9.34 us
    ppermute x1, waiting for transfers between devices, plane_gather(): lax.ppermute(first, 'img', ACROSS_X)  8.7 us
    add x4, other arithmetic, wide(): total = total + part.astype(F32)  8.19 us
    all_to_all x2, starting transfers between devices, to_image(): return lax.all_to_all(parts, 'band', 0, 0, tiled=True).reshape(n, c)  7.05 us
  transfers between devices with their start and end apart: 34, of which 14 were waited for; matrix products, arithmetic and copies ran while one was open for 11% of the time, Pallas kernels for 14%

profile of v1, /device:TPU:0, one launch (start us, length us, event | category | flops | bytes accessed | tf_op | source)
XLA Modules:
  0.0 275.1 jit_solution(12106596811450491133)
XLA Ops:
  7.2 1.1 convert_element_type.221
  8.4 0.9 slice.179
  9.4 3.1 %collective-permute-start = (bf16[64,512]{1,0:T(8,128)(2,1)S(1)}, bf16[64,512]{1,0:T(8,128)(2,1)S(1)}, u32[]{:S(2)}, u32[]{:S(2)}) collective-permute-start(bf16[64,512]{1,0:T(8,128)(2,1)S(1)} %slice.181), channel_id=1, source_target_pairs={{0,8},{4,12},{8,0},{12,4},{16,24},{20,28},{24,16},{28,20},{1,9},{5... | collective-permute-start | bytes 196616 | tf_op jit(solution)/shard_map/ppermute | solution.py:988
  12.5 2.6 collective-permute-start.3
  15.1 3.5 %all-to-all-start = ((bf16[4,256,512]{2,1,0:T(8,128)(2,1)}), bf16[4,256,512]{2,1,0:T(8,128)(2,1)S(1)}, u32[]{:S(2)}, u32[]{:S(2)}) async-start(bf16[4,256,512]{2,1,0:T(8,128)(2,1)} %bitcast.4), calls=%async_computation | async-start | bytes 2097152 | tf_op jit(solution)/shard_map/all_to_all | solution.py:1042
  18.7 2.0 collective-permute-start.1
  21.2 1.6 collective-permute-start.5
  22.7 15.2 %collective-permute-done.1 = bf16[2,64,512]{2,1,0:T(8,128)(2,1)S(1)} collective-permute-done((bf16[2,64,512]{2,1,0:T(8,128)(2,1)S(1)}, bf16[2,64,512]{2,1,0:T(8,128)(2,1)S(1)}, u32[]{:S(2)}, u32[]{:S(2)}) %collective-permute-start.1) | collective-permute-done | bytes 131104 | tf_op jit(solution)/shard_map/ppermute | solution.py:990
  38.0 1.8 collective-permute-start.2
  40.2 8.7 %collective-permute-done.2 = bf16[4,64,512]{2,1,0:T(8,128)(2,1)S(1)} collective-permute-done((bf16[4,64,512]{2,1,0:T(8,128)(2,1)S(1)}, bf16[4,64,512]{2,1,0:T(8,128)(2,1)S(1)}, u32[]{:S(2)}, u32[]{:S(2)}) %collective-permute-start.2) | collective-permute-done | bytes 262176 | tf_op jit(solution)/shard_map/ppermute | solution.py:992
  49.0 2.7 collective-permute-done.6
  51.9 3.5 %all-to-all-start.1 = ((bf16[4,256,512]{2,1,0:T(8,128)(2,1)}), bf16[4,256,512]{2,1,0:T(8,128)(2,1)S(1)}, u32[]{:S(2)}, u32[]{:S(2)}) async-start(bf16[4,256,512]{2,1,0:T(8,128)(2,1)} %bitcast.129), calls=%async_computation.1 | async-start | bytes 2097152 | tf_op jit(solution)/shard_map/all_to_all | solution.py:1042
  55.5 0.6 dynamic_slice.4
  56.1 1.3 stack.41.size_ref.at_ref
  57.4 4.2 %act_one.1 = (bf16[1088,512]{1,0:T(8,128)(2,1)}, bf16[512,1024]{1,0:T(8,128)(2,1)}, f32[8,512]{1,0:T(8,128)}) custom-call(s32[5]{0:T(128)} %stack.41.size_ref.at_ref, bf16[1024,512]{1,0:T(8,128)(2,1)} %bitcast.105, f32[11,512]{1,0:T(8,128)} %vec_ref.7), custom_call_target="tpu_custom_call" | custom-call | tf_op jit(solution)/shard_map/act_one/pallas_call | solution.py:336
  61.6 9.3 %all-to-all-done.1 = bf16[4,256,512]{2,1,0:T(8,128)(2,1)S(1)} async-done(((bf16[4,256,512]{2,1,0:T(8,128)(2,1)}), bf16[4,256,512]{2,1,0:T(8,128)(2,1)S(1)}, u32[]{:S(2)}, u32[]{:S(2)}) %all-to-all-start.1) | async-done | bytes 1048608 | tf_op jit(solution)/shard_map/all_to_all | solution.py:1042
  71.0 28.4 %all-gather.2.cloned.1.call-done.heads_any = bf16[9216,512]{1,0:T(8,128)(2,1)} async-done(((bf16[288,512]{1,0:T(8,128)(2,1)}), bf16[9216,512]{1,0:T(8,128)(2,1)}) %all-gather.2.cloned.1.call-update) | async-done | bytes 9437200 | tf_op jit(solution)/shard_map/all_gather | solution.py:1046
  99.3 44.1 %forward.1 = (bf16[11264,512]{1,0:T(8,128)(2,1)}, f32[1024,512]{1,0:T(8,128)}, f32[8,512]{1,0:T(8,128)}, bf16[1024,512]{1,0:T(8,128)(2,1)}, f32[1024,512]{1,0:T(...) custom-call(s32[5]{0:T(128)} %stack.41.size_ref.at_ref, ...), custom_call_target="tpu_custom_call" | custom-call | tf_op jit(solution)/shard_map/forward/pallas_call | solution.py:336
  144.0 2.9 %collective-permute-done.9 = bf16[8,176,512]{2,1,0:T(8,128)(2,1)S(1)} collective-permute-done((bf16[8,176,512]{2,1,0:T(8,128)(2,1)}, bf16[8,176,512]{2,1,0:T(8,128)(2,1)S(1)}, u32[]{:S(2)}, u32[]{:S(2)}) %collective-permute-start.9) | collective-permute-done | bytes 1441824 | tf_op jit(solution)/shard_map/ppermute | solution.py:967
  146.9 1.8 fusion.refs_2_
  148.7 1.9 collective-permute-start.11
  150.9 0.9 copy-done.19
  152.4 18.8 %back_two.1 = (bf16[1088,1536]{1,0:T(8,128)(2,1)}, f32[8,512]{1,0:T(8,128)}, bf16[8,176,512]{2,1,0:T(8,128)(2,1)}, bf16[8,176,512]{2,1,0:T(8,128)(2,1)}, bf16[8,...) custom-call(s32[5]{0:T(128)} %stack.41.size_ref.at_ref, ...), custom_call_target="tpu_custom_call", output_to_operand_aliasing={{2}: (7, {}), {3}: (8, {}), {4}: (9, {}), {5}: (10, {})} | custom-call | tf_op jit(solution)/shard_map/back_two/pallas_call | solution.py:336
  171.3 0.8 copy-done.1
  173.1 2.8 %collective-permute-done.13 = bf16[8,176,512]{2,1,0:T(8,128)(2,1)} collective-permute-done((bf16[8,176,512]{2,1,0:T(8,128)(2,1)}, bf16[8,176,512]{2,1,0:T(8,128)(2,1)}, u32[]{:S(2)}, u32[]{:S(2)}) %collective-permute-start.13) | collective-permute-done | bytes 1441824 | tf_op jit(solution)/shard_map/ppermute | solution.py:967
  175.9 2.4 fusion.1.refs_2_
  178.3 1.4 collective-permute-start.16
  179.6 2.2 add_convert_fusion.1
  182.1 2.0 fusion.6
  184.1 1.9 collective-permute-start.21
  186.0 2.0 fusion.4
  188.5 15.1 %back_one.1 = (bf16[4,2,256,512]{3,2,1,0:T(8,128)(2,1)}, f32[8,512]{1,0:T(8,128)}) custom-call(s32[5]{0:T(128)} %stack.41.size_ref.at_ref, bf16[1088,1536]{1,0:T(8,128)(2,1)} %after.16.e3_ref, bf16[11264,512]{1,0:T(8,128)(2,1)} %get-tuple-element.44.k_any.k_ref, f32[11,512]{1,0:T(8,128)} %vec_ref.7, bf16[1024,512]{1,0:T(8,128)(2,1)} %bitcast.107, ...), custom_call_target="tpu_custom_call" | custom-call | tf_op jit(solution)/shard_map/back_one/pallas_call | solution.py:336
  203.7 0.7 slice.196
  204.4 0.6 pad_maximum_fusion.6.refs_0_
  205.0 2.1 fusion.9.refs_2_
  207.1 2.0 fusion.10.refs_1_
  209.1 1.5 collective-permute-start.17
  210.5 1.0 collective-permute-start.18
  211.5 1.9 collective-permute-start.19
  213.4 1.4 collective-permute-start.15
  214.8 2.2 fusion.7
  217.0 1.0 collective-permute-start.20
  218.1 2.2 fusion.5
  220.3 0.6 add_add_fusion.1.refs_1_.refs_0_
  220.9 1.3 collective-permute-done.15.refs_0_
  222.3 2.2 fusion.11
  224.5 1.1 collective-permute-done.20.refs_0_
  225.6 1.5 fusion.8
  227.1 1.2 fusion.17
  228.3 1.5 fusion.16
  229.8 0.6 collective-permute-start.23
  230.4 1.9 collective-permute-start.24
  232.3 1.9 collective-permute-start.25
  234.2 3.6 %all-to-all-start.2 = ((bf16[4,2,256,512]{3,2,1,0:T(8,128)(2,1)}), bf16[4,2,256,512]{3,2,1,0:T(8,128)(2,1)S(1)}, u32[]{:S(2)}, u32[]{:S(2)}) async-start(bf16[4,2,256,512]{3,2,1,0:T(8,128)(2,1)} %after.24), calls=%async_computation.2 | async-start | bytes 4194304 | tf_op jit(solution)/shard_map/all_to_all | solution.py:1069
  237.8 6.6 %collective-permute-done.23.refs_1_ = bf16[352,512]{1,0:T(8,128)(2,1)} collective-permute-done((bf16[352,512]{1,0:T(8,128)(2,1)}, bf16[352,512]{1,0:T(8,128)(2,1)}, u32[]{:S(2)}, u32[]{:S(2)}) %collective-permute-start.23) | collective-permute-done | bytes 360480 | tf_op jit(solution)/shard_map/ppermute | solution.py:1014
  244.5 1.5 collective-permute-start.26
  246.0 11.7 %collective-permute-done.24 = bf16[352,512]{1,0:T(8,128)(2,1)} collective-permute-done((bf16[352,512]{1,0:T(8,128)(2,1)S(1)}, bf16[352,512]{1,0:T(8,128)(2,1)}, u32[]{:S(2)}, u32[]{:S(2)}) %collective-permute-start.24) | collective-permute-done | bytes 360480 | tf_op jit(solution)/shard_map/ppermute | solution.py:1014
  257.6 1.9 fusion.14
  260.3 1.1 collective-permute-start.28
  261.4 0.8 collective-permute-start.29
  262.2 1.5 multiply_add_fusion
  264.8 0.7 multiply_add_fusion.2
  265.4 1.2 fusion.20
  266.6 1.6 convert.17
  (131 shorter events, 6.2 us)
Async XLA Ops:
  7.2 92.1 %all-gather.2.cloned.1.call-start = ((), (), s32[]{:S(2)}) async-start(), calls=%async_computation.3 | async-start | bytes 9732096 | tf_op jit(solution)/shard_map/all_gather | solution.py:1046
  9.4 9.3 %collective-permute-start = (bf16[64,512]{1,0:T(8,128)(2,1)S(1)}, bf16[64,512]{1,0:T(8,128)(2,1)S(1)}, u32[]{:S(2)}, u32[]{:S(2)}) collective-permute-start(bf16[64,512]{1,0:T(8,128)(2,1)S(1)} %slice.181), channel_id=1, source_target_pairs={{0,8},{4,12},{8,0},{12,4},{16,24},{20,28},{24,16},{28,20},{1,9},{5... | collective-permute-start | bytes 196616 | tf_op jit(solution)/shard_map/ppermute | solution.py:988
  12.5 8.3 %collective-permute-start.3 = (bf16[64,512]{1,0:T(8,128)(2,1)S(1)}, bf16[64,512]{1,0:T(8,128)(2,1)S(1)}, u32[]{:S(2)}, u32[]{:S(2)}) collective-permute-start(bf16[64,512]{1,0:T(8,128)(2,1)S(1)} %slice.181), channel_id=1, source_target_pairs={{0,16},{4,20},{8,24},{12,28},{16,0},{20,4},{24,8},{28,12},{1,17},{... | collective-permute-start | bytes 196616 | tf_op jit(solution)/shard_map/ppermute | solution.py:988
  15.1 6.1 %collective-permute-start.4 = (bf16[64,512]{1,0:T(8,128)(2,1)S(1)}, bf16[64,512]{1,0:T(8,128)(2,1)S(1)}, u32[]{:S(2)}, u32[]{:S(2)}) collective-permute-start(bf16[64,512]{1,0:T(8,128)(2,1)S(1)} %slice.181), channel_id=1, source_target_pairs={{0,24},{4,28},{8,16},{12,20},{16,8},{20,12},{24,0},{28,4},{1,25},{... | collective-permute-start | bytes 196616 | tf_op jit(solution)/shard_map/ppermute | solution.py:988
  15.1 36.8 %all-to-all-start = ((bf16[4,256,512]{2,1,0:T(8,128)(2,1)}), bf16[4,256,512]{2,1,0:T(8,128)(2,1)S(1)}, u32[]{:S(2)}, u32[]{:S(2)}) async-start(bf16[4,256,512]{2,1,0:T(8,128)(2,1)} %bitcast.4), calls=%async_computation | async-start | bytes 2097152 | tf_op jit(solution)/shard_map/all_to_all | solution.py:1042
  18.7 19.3 %collective-permute-start.1 = (bf16[2,64,512]{2,1,0:T(8,128)(2,1)S(1)}, bf16[2,64,512]{2,1,0:T(8,128)(2,1)S(1)}, u32[]{:S(2)}, u32[]{:S(2)}) collective-permute-start(bf16[2,64,512]{2,1,0:T(8,128)(2,1)S(1)} %pad_maximum_fusion.4), channel_id=1, source_target_pairs={{0,2},{1,3},{2,0},{3,1},{4,6},{5,7},{6,4},{7,5},{8,10},{9,11},{10,... | collective-permute-start | bytes 393224 | tf_op jit(solution)/shard_map/ppermute | solution.py:990
  21.2 18.6 %collective-permute-start.5 = (bf16[2,64,512]{2,1,0:T(8,128)(2,1)S(1)}, bf16[2,64,512]{2,1,0:T(8,128)(2,1)S(1)}, u32[]{:S(2)}, u32[]{:S(2)}) collective-permute-start(bf16[2,64,512]{2,1,0:T(8,128)(2,1)S(1)} %pad_maximum_fusion.5), channel_id=1, source_target_pairs={{0,4},{4,0},{8,12},{12,8},{16,20},{20,16},{24,28},{28,24},{1,5},{5... | collective-permute-start | bytes 393224 | tf_op jit(solution)/shard_map/ppermute | solution.py:991
  38.0 11.0 %collective-permute-start.2 = (bf16[4,64,512]{2,1,0:T(8,128)(2,1)S(1)}, bf16[4,64,512]{2,1,0:T(8,128)(2,1)S(1)}, u32[]{:S(2)}, u32[]{:S(2)}) collective-permute-start(bf16[4,64,512]{2,1,0:T(8,128)(2,1)S(1)} %pad_maximum_fusion.2), channel_id=1, source_target_pairs={{0,4},{4,0},{8,12},{12,8},{16,20},{20,16},{24,28},{28,24},{1,5},{5... | collective-permute-start | bytes 786440 | tf_op jit(solution)/shard_map/ppermute | solution.py:992
  39.8 12.0 %collective-permute-start.6 = (bf16[4,64,512]{2,1,0:T(8,128)(2,1)S(1)}, bf16[4,64,512]{2,1,0:T(8,128)(2,1)S(1)}, u32[]{:S(2)}, u32[]{:S(2)}) collective-permute-start(bf16[4,64,512]{2,1,0:T(8,128)(2,1)S(1)} %pad_maximum_fusion.3), channel_id=1, source_target_pairs={{0,2},{1,3},{2,0},{3,1},{4,6},{5,7},{6,4},{7,5},{8,10},{9,11},{10,... | collective-permute-start | bytes 786440 | tf_op jit(solution)/shard_map/ppermute | solution.py:992
  49.0 6.5 %copy-start.31 = (s32[4]{0:T(128)S(1)}, s32[4]{0:T(128)}, u32[]{:S(2)}) copy-start(s32[4]{0:T(128)} %param.11) | copy-start | bytes 52
  51.8 9.8 %copy-start.21 = (bf16[16,64,512]{2,1,0:T(8,128)(2,1)}, bf16[16,64,512]{2,1,0:T(8,128)(2,1)S(1)}, u32[]{:S(2)}) copy-start(bf16[16,64,512]{2,1,0:T(8,128)(2,1)S(1)} %constant_dynamic-update-slice_fusion.mine_any) | copy-start | bytes 3145732
  51.8 19.2 %collective-permute-start.7 = (bf16[16,64,512]{2,1,0:T(8,128)(2,1)S(1)}, bf16[16,64,512]{2,1,0:T(8,128)(2,1)}, u32[]{:S(2)}, u32[]{:S(2)}) collective-permute-start(bf16[16,64,512]{2,1,0:T(8,128)(2,1)S(1)} %constant_dynamic-update-slice_fusion.mine_any), channel_id=1, source_target_pairs={{0,1},{1,0},{2,3},{3,2},{4,5},{5,4},{6,7},{7,6},{8,9},{9,8},{10,11... | collective-permute-start | bytes 3145736 | tf_op jit(solution)/shard_map/ppermute | solution.py:993
  51.9 5.5 %copy-start = (bf16[4,256,512]{2,1,0:T(8,128)(2,1)}, bf16[4,256,512]{2,1,0:T(8,128)(2,1)S(1)}, u32[]{:S(2)}) copy-start(bf16[4,256,512]{2,1,0:T(8,128)(2,1)S(1)} %all-to-all-done) | copy-start | bytes 3145732
  51.9 19.1 %all-to-all-start.1 = ((bf16[4,256,512]{2,1,0:T(8,128)(2,1)}), bf16[4,256,512]{2,1,0:T(8,128)(2,1)S(1)}, u32[]{:S(2)}, u32[]{:S(2)}) async-start(bf16[4,256,512]{2,1,0:T(8,128)(2,1)} %bitcast.129), calls=%async_computation.1 | async-start | bytes 2097152 | tf_op jit(solution)/shard_map/all_to_all | solution.py:1042
  71.0 28.4 %copy-start.9 = (bf16[4,256,512]{2,1,0:T(8,128)(2,1)}, bf16[4,256,512]{2,1,0:T(8,128)(2,1)S(1)}, u32[]{:S(2)}) copy-start(bf16[4,256,512]{2,1,0:T(8,128)(2,1)S(1)} %all-to-all-done.1) | copy-start | bytes 3145732
  143.4 7.3 %copy-start.18 = (bf16[8,176,512]{2,1,0:T(8,128)(2,1)S(1)}, bf16[8,176,512]{2,1,0:T(8,128)(2,1)}, u32[]{:S(2)}) copy-start(bf16[8,176,512]{2,1,0:T(8,128)(2,1)} %get-tuple-element.39) | copy-start | bytes 4325380
  143.4 3.5 %collective-permute-start.9 = (bf16[8,176,512]{2,1,0:T(8,128)(2,1)}, bf16[8,176,512]{2,1,0:T(8,128)(2,1)S(1)}, u32[]{:S(2)}, u32[]{:S(2)}) collective-permute-start(bf16[8,176,512]{2,1,0:T(8,128)(2,1)} %get-tuple-element.42), channel_id=1, source_target_pairs={{0,1},{1,0},{2,3},{3,2},{4,5},{5,4},{6,7},{7,6},{8,9},{9,8},{10,11... | collective-permute-start | bytes 4325384 | tf_op jit(solution)/shard_map/ppermute | solution.py:967
  143.8 6.9 %collective-permute-start.8 = (bf16[8,176,512]{2,1,0:T(8,128)(2,1)}, bf16[8,176,512]{2,1,0:T(8,128)(2,1)S(1)}, u32[]{:S(2)}, u32[]{:S(2)}) collective-permute-start(bf16[8,176,512]{2,1,0:T(8,128)(2,1)} %get-tuple-element.40), channel_id=1, source_target_pairs={{0,1},{1,0},{2,3},{3,2},{4,5},{5,4},{6,7},{7,6},{8,9},{9,8},{10,11... | collective-permute-start | bytes 4325384 | tf_op jit(solution)/shard_map/ppermute | solution.py:967
  146.9 4.0 %copy-start.17 = (bf16[8,176,512]{2,1,0:T(8,128)(2,1)}, bf16[8,176,512]{2,1,0:T(8,128)(2,1)S(1)}, u32[]{:S(2)}) copy-start(bf16[8,176,512]{2,1,0:T(8,128)(2,1)S(1)} %collective-permute-done.9) | copy-start | bytes 4325380
  148.7 3.7 %copy-start.15 = (bf16[2,2,176,512]{3,2,1,0:T(8,128)(2,1)}, bf16[2,2,176,512]{3,2,1,0:T(8,128)(2,1)S(1)}, u32[]{:S(2)}) copy-start(bf16[2,2,176,512]{3,2,1,0:T(8,128)(2,1)S(1)} %fusion.refs_2_) | copy-start | bytes 2162692
  148.7 22.5 %collective-permute-start.11 = (bf16[2,2,176,512]{3,2,1,0:T(8,128)(2,1)S(1)}, bf16[2,2,176,512]{3,2,1,0:T(8,128)(2,1)S(1)}, u32[]{:S(2)}, u32[]{:S(2)}) collective-permute-start(bf16[2,2,176,512]{3,2,1,0:T(8,128)(2,1)S(1)} %fusion.refs_2_), channel_id=1, source_target_pairs={{0,2},{1,3},{2,0},{3,1},{4,6},{5,7},{6,4},{7,5},{8,10},{9,11},{10,... | collective-permute-start | bytes 2162696 | tf_op jit(solution)/shard_map/ppermute | solution.py:976
  150.7 1.1 copy-start.19
  150.9 1.5 copy-start.16
  151.8 19.5 %collective-permute-start.10 = (bf16[2,2,176,512]{3,2,1,0:T(8,128)(2,1)S(1)}, bf16[2,2,176,512]{3,2,1,0:T(8,128)(2,1)S(1)}, u32[]{:S(2)}, u32[]{:S(2)}) collective-permute-start(bf16[2,2,176,512]{3,2,1,0:T(8,128)(2,1)S(1)} %bitcast.117), channel_id=1, source_target_pairs={{0,4},{4,0},{8,12},{12,8},{16,20},{20,16},{24,28},{28,24},{1,5},{5... | collective-permute-start | bytes 2162696 | tf_op jit(solution)/shard_map/ppermute | solution.py:976
  171.2 0.9 copy-start.1
  171.3 1.1 copy-start.3
  172.3 3.6 %collective-permute-start.13 = (bf16[8,176,512]{2,1,0:T(8,128)(2,1)}, bf16[8,176,512]{2,1,0:T(8,128)(2,1)}, u32[]{:S(2)}, u32[]{:S(2)}) collective-permute-start(bf16[8,176,512]{2,1,0:T(8,128)(2,1)} %after.15), channel_id=1, source_target_pairs={{0,1},{1,0},{2,3},{3,2},{4,5},{5,4},{6,7},{7,6},{8,9},{9,8},{10,11... | collective-permute-start | bytes 4325384 | tf_op jit(solution)/shard_map/ppermute | solution.py:967
  172.3 7.3 %copy-start.8 = (bf16[8,176,512]{2,1,0:T(8,128)(2,1)S(1)}, bf16[8,176,512]{2,1,0:T(8,128)(2,1)}, u32[]{:S(2)}) copy-start(bf16[8,176,512]{2,1,0:T(8,128)(2,1)} %get-tuple-element.52) | copy-start | bytes 4325380
  172.3 7.3 %collective-permute-start.12 = (bf16[8,176,512]{2,1,0:T(8,128)(2,1)}, bf16[8,176,512]{2,1,0:T(8,128)(2,1)}, u32[]{:S(2)}, u32[]{:S(2)}) collective-permute-start(bf16[8,176,512]{2,1,0:T(8,128)(2,1)} %after.14), channel_id=1, source_target_pairs={{0,1},{1,0},{2,3},{3,2},{4,5},{5,4},{6,7},{7,6},{8,9},{9,8},{10,11... | collective-permute-start | bytes 4325384 | tf_op jit(solution)/shard_map/ppermute | solution.py:967
  178.3 3.9 %copy-start.4 = (bf16[2,2,176,512]{3,2,1,0:T(8,128)(2,1)S(1)}, bf16[2,2,176,512]{3,2,1,0:T(8,128)(2,1)}, u32[]{:S(2)}) copy-start(bf16[2,2,176,512]{3,2,1,0:T(8,128)(2,1)} %copy-done.3) | copy-start | bytes 2162692
  178.3 26.7 %collective-permute-start.16 = (bf16[2,2,176,512]{3,2,1,0:T(8,128)(2,1)}, bf16[2,2,176,512]{3,2,1,0:T(8,128)(2,1)}, u32[]{:S(2)}, u32[]{:S(2)}) collective-permute-start(bf16[2,2,176,512]{3,2,1,0:T(8,128)(2,1)} %fusion.1.refs_2_), channel_id=1, source_target_pairs={{0,2},{1,3},{2,0},{3,1},{4,6},{5,7},{6,4},{7,5},{8,10},{9,11},{10,... | collective-permute-start | bytes 2162696 | tf_op jit(solution)/shard_map/ppermute | solution.py:976
  179.6 6.3 %copy-start.2 = (bf16[2,2,176,512]{3,2,1,0:T(8,128)(2,1)S(1)}, bf16[2,2,176,512]{3,2,1,0:T(8,128)(2,1)}, u32[]{:S(2)}) copy-start(bf16[2,2,176,512]{3,2,1,0:T(8,128)(2,1)} %copy-done.1) | copy-start | bytes 2162692
  181.9 25.2 %collective-permute-start.14 = (bf16[2,2,176,512]{3,2,1,0:T(8,128)(2,1)}, bf16[2,2,176,512]{3,2,1,0:T(8,128)(2,1)}, u32[]{:S(2)}, u32[]{:S(2)}) collective-permute-start(bf16[2,2,176,512]{3,2,1,0:T(8,128)(2,1)} %bitcast.15.refs_1_), channel_id=1, source_target_pairs={{0,4},{4,0},{8,12},{12,8},{16,20},{20,16},{24,28},{28,24},{1,5},{5... | collective-permute-start | bytes 2162696 | tf_op jit(solution)/shard_map/ppermute | solution.py:976
  184.1 29.3 %collective-permute-start.21 = (bf16[2,176,512]{2,1,0:T(8,128)(2,1)}, bf16[2,176,512]{2,1,0:T(8,128)(2,1)}, u32[]{:S(2)}, u32[]{:S(2)}) collective-permute-start(bf16[2,176,512]{2,1,0:T(8,128)(2,1)} %fusion.6), channel_id=1, source_target_pairs={{0,2},{1,3},{2,0},{3,1},{4,6},{5,7},{6,4},{7,5},{8,10},{9,11},{10,... | collective-permute-start | bytes 1081352 | tf_op jit(solution)/shard_map/ppermute | solution.py:997
  187.9 29.1 %collective-permute-start.22 = (bf16[2,176,512]{2,1,0:T(8,128)(2,1)}, bf16[2,176,512]{2,1,0:T(8,128)(2,1)}, u32[]{:S(2)}, u32[]{:S(2)}) collective-permute-start(bf16[2,176,512]{2,1,0:T(8,128)(2,1)} %fusion.4), channel_id=1, source_target_pairs={{0,4},{4,0},{8,12},{12,8},{16,20},{20,16},{24,28},{28,24},{1,5},{5... | collective-permute-start | bytes 1081352 | tf_op jit(solution)/shard_map/ppermute | solution.py:998
  188.5 15.9 %copy-start.29 = (f32[8,512]{1,0:T(8,128)S(1)}, f32[8,512]{1,0:T(8,128)}, u32[]{:S(2)}) copy-start(f32[8,512]{1,0:T(8,128)} %get-tuple-element.63) | copy-start | bytes 49156
  209.1 11.2 %collective-permute-start.17 = (f32[11,512]{1,0:T(8,128)}, f32[11,512]{1,0:T(8,128)S(1)}, u32[]{:S(2)}, u32[]{:S(2)}) collective-permute-start(f32[11,512]{1,0:T(8,128)} %after.19), channel_id=1, source_target_pairs={{0,8},{4,12},{8,0},{12,4},{16,24},{20,28},{24,16},{28,20},{1,9},{5... | collective-permute-start | bytes 67592 | tf_op jit(solution)/shard_map/ppermute | solution.py:1019
  210.5 9.8 %collective-permute-start.18 = (f32[11,512]{1,0:T(8,128)}, f32[11,512]{1,0:T(8,128)S(1)}, u32[]{:S(2)}, u32[]{:S(2)}) collective-permute-start(f32[11,512]{1,0:T(8,128)} %after.19), channel_id=1, source_target_pairs={{0,16},{4,20},{8,24},{12,28},{16,0},{20,4},{24,8},{28,12},{1,17},{... | collective-permute-start | bytes 67592 | tf_op jit(solution)/shard_map/ppermute | solution.py:1019
  211.5 8.8 %collective-permute-start.19 = (f32[11,512]{1,0:T(8,128)}, f32[11,512]{1,0:T(8,128)S(1)}, u32[]{:S(2)}, u32[]{:S(2)}) collective-permute-start(f32[11,512]{1,0:T(8,128)} %after.19), channel_id=1, source_target_pairs={{0,24},{4,28},{8,16},{12,20},{16,8},{20,12},{24,0},{28,4},{1,25},{... | collective-permute-start | bytes 67592 | tf_op jit(solution)/shard_map/ppermute | solution.py:1019
  213.4 8.8 %collective-permute-start.15 = (bf16[2,176,512]{2,1,0:T(8,128)(2,1)}, bf16[2,176,512]{2,1,0:T(8,128)(2,1)}, u32[]{:S(2)}, u32[]{:S(2)}) collective-permute-start(bf16[2,176,512]{2,1,0:T(8,128)(2,1)} %fusion.10.refs_1_), channel_id=1, source_target_pairs={{0,2},{1,3},{2,0},{3,1},{4,6},{5,7},{6,4},{7,5},{8,10},{9,11},{10,... | collective-permute-start | bytes 1081352 | tf_op jit(solution)/shard_map/ppermute | solution.py:997
  217.0 3.3 %copy-start.26 = (f32[11,512]{1,0:T(8,128)S(1)}, f32[11,512]{1,0:T(8,128)}, u32[]{:S(2)}) copy-start(f32[11,512]{1,0:T(8,128)} %after.19) | copy-start | bytes 67588
  217.0 8.5 %collective-permute-start.20 = (bf16[2,176,512]{2,1,0:T(8,128)(2,1)}, bf16[2,176,512]{2,1,0:T(8,128)(2,1)}, u32[]{:S(2)}, u32[]{:S(2)}) collective-permute-start(bf16[2,176,512]{2,1,0:T(8,128)(2,1)} %fusion.9.refs_2_), channel_id=1, source_target_pairs={{0,4},{4,0},{8,12},{12,8},{16,20},{20,16},{24,28},{28,24},{1,5},{5... | collective-permute-start | bytes 1081352 | tf_op jit(solution)/shard_map/ppermute | solution.py:998
  224.5 2.6 copy-start.12
  224.5 2.6 copy-start.13
  224.5 2.6 copy-start.14
  228.3 1.5 copy-start.5
  228.3 1.5 copy-start.6
  228.3 1.5 copy-start.7
  229.8 4.5 %copy-start.20 = (bf16[352,512]{1,0:T(8,128)(2,1)}, bf16[352,512]{1,0:T(8,128)(2,1)S(1)}, u32[]{:S(2)}) copy-start(bf16[352,512]{1,0:T(8,128)(2,1)S(1)} %get-tuple-element.76.refs_2_) | copy-start | bytes 1081348
  229.8 14.7 %collective-permute-start.23 = (bf16[352,512]{1,0:T(8,128)(2,1)}, bf16[352,512]{1,0:T(8,128)(2,1)}, u32[]{:S(2)}, u32[]{:S(2)}) collective-permute-start(bf16[352,512]{1,0:T(8,128)(2,1)} %get-tuple-element.77.refs_1_), channel_id=1, source_target_pairs={{0,8},{4,12},{8,0},{12,4},{16,24},{20,28},{24,16},{28,20},{1,9},{5... | collective-permute-start | bytes 1081352 | tf_op jit(solution)/shard_map/ppermute | solution.py:1014
  230.4 27.2 %collective-permute-start.24 = (bf16[352,512]{1,0:T(8,128)(2,1)S(1)}, bf16[352,512]{1,0:T(8,128)(2,1)}, u32[]{:S(2)}, u32[]{:S(2)}) collective-permute-start(bf16[352,512]{1,0:T(8,128)(2,1)S(1)} %get-tuple-element.76.refs_2_), channel_id=1, source_target_pairs={{0,16},{4,20},{8,24},{12,28},{16,0},{20,4},{24,8},{28,12},{1,17},{... | collective-permute-start | bytes 1081352 | tf_op jit(solution)/shard_map/ppermute | solution.py:1014
  232.3 25.3 %collective-permute-start.25 = (bf16[352,512]{1,0:T(8,128)(2,1)}, bf16[352,512]{1,0:T(8,128)(2,1)}, u32[]{:S(2)}, u32[]{:S(2)}) collective-permute-start(bf16[352,512]{1,0:T(8,128)(2,1)} %get-tuple-element.71.refs_3_), channel_id=1, source_target_pairs={{0,24},{4,28},{8,16},{12,20},{16,8},{20,12},{24,0},{28,4},{1,25},{... | collective-permute-start | bytes 1081352 | tf_op jit(solution)/shard_map/ppermute | solution.py:1014
  234.2 31.2 %all-to-all-start.2 = ((bf16[4,2,256,512]{3,2,1,0:T(8,128)(2,1)}), bf16[4,2,256,512]{3,2,1,0:T(8,128)(2,1)S(1)}, u32[]{:S(2)}, u32[]{:S(2)}) async-start(bf16[4,2,256,512]{3,2,1,0:T(8,128)(2,1)} %after.24), calls=%async_computation.2 | async-start | bytes 4194304 | tf_op jit(solution)/shard_map/all_to_all | solution.py:1069
  244.5 15.4 %collective-permute-start.26 = (f32[11,512]{1,0:T(8,128)}, f32[11,512]{1,0:T(8,128)S(1)}, u32[]{:S(2)}, u32[]{:S(2)}) collective-permute-start(f32[11,512]{1,0:T(8,128)} %after.25), channel_id=1, source_target_pairs={{0,4},{4,0},{8,12},{12,8},{16,20},{20,16},{24,28},{28,24},{1,5},{5... | collective-permute-start | bytes 67592 | tf_op jit(solution)/shard_map/ppermute | solution.py:1073
  257.6 4.6 %copy-start.25 = (f32[180224]{0:T(1024)S(1)}, f32[180224]{0:T(1024)}, u32[]{:S(2)}) copy-start(f32[180224]{0:T(1024)} %param.13) | copy-start | bytes 2162692
  259.6 2.6 copy-start.10
  259.6 2.6 copy-start.24
  259.8 4.0 %copy-start.11 = (f32[44,4,8,128]{3,1,2,0:T(4,128)}, f32[44,4,8,128]{3,1,2,0:T(4,128)S(1)}, u32[]{:S(2)}) copy-start(f32[44,4,8,128]{3,1,2,0:T(4,128)S(1)} %copy.36) | copy-start | bytes 2162692
  260.3 3.4 %collective-permute-start.27 = (f32[11,512]{1,0:T(8,128)S(1)}, f32[11,512]{1,0:T(8,128)S(1)}, u32[]{:S(2)}, u32[]{:S(2)}) collective-permute-start(f32[11,512]{1,0:T(8,128)S(1)} %add.205), channel_id=1, source_target_pairs={{0,1},{1,0},{2,3},{3,2},{4,5},{5,4},{6,7},{7,6},{8,9},{9,8},{10,11... | collective-permute-start | bytes 67592 | tf_op jit(solution)/shard_map/ppermute | solution.py:1019
  260.3 4.0 %collective-permute-start.28 = (f32[11,512]{1,0:T(8,128)S(1)}, f32[11,512]{1,0:T(8,128)S(1)}, u32[]{:S(2)}, u32[]{:S(2)}) collective-permute-start(f32[11,512]{1,0:T(8,128)S(1)} %add.205), channel_id=1, source_target_pairs={{0,2},{1,3},{2,0},{3,1},{4,6},{5,7},{6,4},{7,5},{8,10},{9,11},{10,... | collective-permute-start | bytes 67592 | tf_op jit(solution)/shard_map/ppermute | solution.py:1019
  261.4 3.4 %collective-permute-start.29 = (f32[11,512]{1,0:T(8,128)S(1)}, f32[11,512]{1,0:T(8,128)S(1)}, u32[]{:S(2)}, u32[]{:S(2)}) collective-permute-start(f32[11,512]{1,0:T(8,128)S(1)} %add.205), channel_id=1, source_target_pairs={{0,3},{1,2},{2,1},{3,0},{4,7},{5,6},{6,5},{7,4},{8,11},{9,10},{10,... | collective-permute-start | bytes 67592 | tf_op jit(solution)/shard_map/ppermute | solution.py:1019
  262.2 2.6 copy-start.22
  262.2 2.5 copy-start.27
  262.2 2.5 copy-start.28
  (2 other events, 1.5 us)
Sparse Core Ops, SparseCore 0:
  11.5 87.7 all-gather.1
